TPU v7x, 128 devices: a whole 4x4x4 slice. The times are simulated.
128 devices in a mesh: dp: 16 (over y_hi, x, core), tensor: 8 (over z, y_lo).
Axes of the slice: x: 4, y: 4 (y_hi: 2, y_lo: 2; y = y_hi * 2 + y_lo), z: 4, core: 2. Of those that a mesh axis runs over, the one named last changes fastest.
Arguments:
- tokens: bfloat16 [32768, 1536], P('dp'), may hold values from -6 to 6
- w_in: bfloat16 [1536, 6144], P(None, 'tensor'), may hold values from -0.15625 to 0.15625
- w_out: bfloat16 [6144, 1536], P('tensor'), may hold values from -0.078125 to 0.078125
- text_emb: bfloat16 [128, 1536], P('dp'), may hold values from -6 to 6
- labels: int32 [128], P('dp'), may hold values from 0 to 127, each once
- logit_scale: float32 [1], replicated, may hold values from 2 to 8
- logit_bias: float32 [1], replicated, may hold values from -1.5 to 0.5
Outputs:
- token_grad: bfloat16 [32768, 1536], P('dp', 'tensor')
- w_in_grad: bfloat16 [1536, 6144], P('dp', 'tensor')
- w_out_grad: bfloat16 [6144, 1536], P('tensor', 'dp')
- text_grad: bfloat16 [128, 1536], P('dp')
Inputs may be any that keep to these rules, and one draw needn't show every extreme that they name: `labels`: each text index appears exactly once.
All inputs are finite; a program needn't handle non-finite values.
Results may differ from a plain program's by a relative error of at most 0.015.
Values may be sent and summed in bfloat16 or wider, within the bound.
A program may use at most 128 MiB of HBM per device.

v0:
```python
import jax
import jax.numpy as jnp
from jax import lax
from jax.sharding import PartitionSpec as P

TOKS = 256


loss_scale = 8192.0
norm_eps = 1e-06


def shifted(block, axis, distance):
    devices = range(lax.axis_size(axis))
    route = [((i - distance) % len(devices), i) for i in devices]
    return lax.ppermute(block, axis, route)


def layer_stats(block):
    values = block.astype(jnp.float32)
    center = values - jnp.mean(values, axis=1, keepdims=True)
    inv_std = lax.rsqrt(jnp.mean(center * center, axis=1, keepdims=True) + norm_eps)
    return (center * inv_std, inv_std)


def sig_grads(image_bf, text_bf, match, logit_scale, logit_bias, count):
    logits = (
        logit_scale[0] * jnp.dot(image_bf, text_bf.T, preferred_element_type=jnp.float32)
        + logit_bias[0]
    )
    signs = jnp.where(match, 1.0, -1.0).astype(logits.dtype)
    grad_logit = -signs * jax.nn.sigmoid(-signs * logits) * (loss_scale / count)
    return grad_logit.astype(jnp.bfloat16)


def body(tokens, w_in, w_out, text_emb, labels, logit_scale, logit_bias):
    groups = lax.axis_size("dp")
    position = lax.axis_index("dp")
    parts = lax.axis_size("tensor")
    part_index = lax.axis_index("tensor")
    local_images = text_emb.shape[0]
    images_all = local_images * groups
    block_rows = tokens.shape[0]
    width = tokens.shape[1]
    normed, inv_std = layer_stats(tokens)
    normed_bf = normed.astype(jnp.bfloat16)
    hidden_pre = jnp.dot(normed_bf, w_in, preferred_element_type=jnp.float32)
    hidden_width = hidden_pre.shape[1]
    pooled = jnp.mean(jax.nn.gelu(hidden_pre).reshape(local_images, TOKS, hidden_width), axis=1)
    pooled_bf = pooled.astype(jnp.bfloat16)
    token_mean = jnp.mean(tokens.astype(jnp.float32).reshape(local_images, TOKS, width), axis=1)
    embedding = token_mean + lax.psum(
        jnp.dot(pooled_bf, w_out, preferred_element_type=jnp.float32), "tensor"
    )
    emb_inv = lax.rsqrt(jnp.sum(embedding * embedding, axis=1, keepdims=True) + norm_eps)
    image_bf = (embedding * emb_inv).astype(jnp.bfloat16)
    text_vals = text_emb.astype(jnp.float32)
    text_inv = lax.rsqrt(jnp.sum(text_vals * text_vals, axis=1, keepdims=True) + norm_eps)
    text_bf = (text_vals * text_inv).astype(jnp.bfloat16)

    def turn_step(turn, carry):
        image_acc, visit_text, visit_grad = carry
        owner = (position - turn) % groups
        columns = owner * local_images + jnp.arange(local_images, dtype=jnp.int32)
        match = labels[:, None] == columns[None, :]
        grad_bf = sig_grads(image_bf, visit_text, match, logit_scale, logit_bias, images_all)
        image_acc = image_acc + logit_scale[0] * jnp.dot(
            grad_bf, visit_text, preferred_element_type=jnp.float32
        )
        visit_grad = visit_grad + logit_scale[0] * jnp.dot(
            grad_bf.T, image_bf, preferred_element_type=jnp.float32
        )
        visit_text = shifted(visit_text, "dp", 1)
        visit_grad = shifted(visit_grad, "dp", 1)
        return (image_acc, visit_text, visit_grad)

    start_state = (
        jnp.zeros((local_images, width), jnp.float32),
        text_bf,
        jnp.zeros((local_images, width), jnp.float32),
    )
    image_dir, unused_text, text_dir = lax.fori_loop(0, groups, turn_step, start_state)
    emb_grad = emb_inv * image_dir - emb_inv**3 * embedding * jnp.sum(
        embedding * image_dir, axis=1, keepdims=True
    )
    text_grad = (
        text_inv * text_dir
        - text_inv**3 * text_vals * jnp.sum(text_vals * text_dir, axis=1, keepdims=True)
    ).astype(jnp.bfloat16)
    emb_grad_bf = emb_grad.astype(jnp.bfloat16)
    pooled_grad = jnp.einsum("id,fd->if", emb_grad_bf, w_out, preferred_element_type=jnp.float32)
    w_out_part = jnp.einsum("if,id->fd", pooled_bf, emb_grad_bf, preferred_element_type=jnp.float32)
    spread = jnp.broadcast_to(
        (pooled_grad / TOKS)[:, None, :], (local_images, TOKS, hidden_width)
    ).reshape(block_rows, hidden_width)
    hidden_grad = jax.vjp(jax.nn.gelu, hidden_pre)[1](spread)[0].astype(jnp.bfloat16)
    w_in_part = jnp.einsum("rd,rf->df", normed_bf, hidden_grad, preferred_element_type=jnp.float32)
    w_in_grad, w_out_grad = (
        lax.psum_scatter(w_in_part, "dp", scatter_dimension=0, tiled=True),
        lax.psum_scatter(w_out_part, "dp", scatter_dimension=1, tiled=True),
    )
    piece = width // parts
    col_start = part_index * piece
    partial_feats = jnp.einsum("rf,df->rd", hidden_grad, w_in, preferred_element_type=jnp.float32)
    summed = lax.psum_scatter(
        partial_feats.astype(jnp.bfloat16), "tensor", scatter_dimension=1, tiled=True
    ).astype(jnp.float32)
    normed_cols = lax.dynamic_slice_in_dim(normed, col_start, piece, 1)
    first_sum, second_sum = lax.psum(
        (jnp.sum(summed, axis=1), jnp.sum(summed * normed_cols, axis=1)), "tensor"
    )
    emb_cols = lax.dynamic_slice_in_dim(emb_grad, col_start, piece, 1)
    emb_spread = jnp.broadcast_to(
        (emb_cols / TOKS)[:, None, :], (local_images, TOKS, piece)
    ).reshape(block_rows, piece)
    grad_cols = (
        inv_std * (summed - first_sum[:, None] / width - normed_cols * second_sum[:, None] / width)
        + emb_spread
    )
    token_grad = grad_cols.astype(jnp.bfloat16)
    return (token_grad, w_in_grad.astype(jnp.bfloat16), w_out_grad.astype(jnp.bfloat16), text_grad)


def solution(mesh):
    in_specs = (
        P("dp", None),
        P(None, "tensor"),
        P("tensor", None),
        P("dp", None),
        P("dp"),
        P(),
        P(),
    )
    out_specs = (P("dp", "tensor"), P("dp", "tensor"), P("tensor", "dp"), P("dp", None))
    return jax.shard_map(body, mesh=mesh, in_specs=in_specs, out_specs=out_specs, check_vma=False)
```

profile of v0, /device:TPU:0, one launch (start us, length us, event | category | flops | bytes accessed | tf_op | source)
XLA Modules:
  0.0 608.7 jit_solution(14929682526947371466)
XLA Ops:
  7.2 8.9 %copy.13 = bf16[2048,1536]{0,1:T(8,128)(2,1)} copy(bf16[2048,1536]{1,0:T(8,128)(2,1)} %param.9) | data formatting | bytes 12582912 | tf_op args[0]
  16.1 4.1 convert_reduce_fusion
  20.7 6.1 convert_element_type.53
  26.8 4.6 multiply_reduce_fusion
  31.4 8.6 %bitcast_reduce_fusion = (f32[8,768]{1,0:T(8,128)S(1)}, f32[2048,768]{1,0:T(8,128)}) fusion(bf16[1536,768]{1,0:T(8,128)(2,1)S(1)} %copy-done, f32[2048]{0:T(1024)S(1)} %add_rsqrt_fusion, f32[2048]{0:T(1024)S(1)} %broadcast_multiply_fusion.1, bf16[2048,1536]{0,1:T(8,128)(2,1)S(1)} %copy-done.2), kind=kOutput, calls=%fused_computation.33 | convolution fusion | flops 4858570752 | bytes 14983168 | tf_op jit(solution)/shard_map/dot_general | solution.py:47
  40.5 36.4 %psum.21 = f32[8,1536]{1,0:T(8,128)S(1)} all-reduce(f32[8,1536]{1,0:T(8,128)S(1)} %fusion.39), channel_id=1, replica_groups=mesh['dp'=16,'tensor'=8] {'tensor'}, use_global_device_ids=true, to_apply=%region_4.0 | all-reduce | flops 12288 | bytes 98304 | tf_op jit(solution)/shard_map/psum | solution.py:52
  76.9 15.3 %copy.16 = f32[192,8,8,256]{3,2,1,0:T(8,128)} copy(f32[192,8,8,256]{3,1,2,0:T(8,128)} %bitcast.55) | data formatting | bytes 25165824
  92.2 6.3 %reduce_sum.92 = f32[8,1536]{0,1:T(8,128)S(1)} reduce(f32[8,256,1536]{1,0,2:T(8,128)} %bitcast.56, f32[]{:T(128)} %constant.111.clone.1), dimensions={1}, to_apply=%region_2.0 | reduce | flops 3133440 | bytes 12632068 | tf_op jit(solution)/shard_map/reduce_sum | solution.py:51
  99.1 150.8 %while.20 = (s32[]{:T(128)}, f32[8,1536]{1,0:T(8,128)S(1)}, bf16[8,1536]{1,0:T(8,128)(2,1)S(1)}, f32[8,1536]{1,0:T(8,128)S(1)}, f32[1]{0:T(128)}, /*index=5*/s32...) while((s32[]{:T(128)}, f32[8,1536]{1,0:T(8,128)S(1)}, ...), condition=%wide.region_8.9_spmd.clone, body=%wide.region_7.8_spmd.clone.sunk | while | flops 652056 | bytes 639832 | solution.py:82
  111.8 3.8 collective-permute-done
  121.2 3.8 collective-permute-done
  130.6 3.8 collective-permute-done
  140.0 3.8 collective-permute-done
  149.4 3.8 collective-permute-done
  187.1 3.8 collective-permute-done
  224.8 3.8 collective-permute-done
  252.7 6.3 %fusion.17 = bf16[2048,768]{1,0:T(8,128)(2,1)S(1)} fusion(f32[2048,768]{1,0:T(8,128)} %get-tuple-element.287, f32[8,768]{1,0:T(8,128)S(1)} %convolution_multiply_fusion.3), kind=kLoop, calls=%fused_computation.29 | loop fusion | flops 31457280 | bytes 9461760 | tf_op jit(solution)/shard_map/convert_element_type | solution.py:96
  260.7 6.7 %fusion.21 = f32[1536,768]{1,0:T(8,128)} fusion(bf16[2048,768]{1,0:T(8,128)(2,1)S(1)} %fusion.17, bf16[2048,1536]{0,1:T(8,128)(2,1)S(1)} %bitcast.54, f32[2048]{0:T(1024)S(1)} %add_rsqrt_fusion, f32[2048]{0:T(1024)S(1)} %broadcast_multiply_fusion.1), kind=kOutput, calls=%fused_computation.35 | convolution fusion | flops 4844421120 | bytes 14172160 | tf_op jit(solution)/shard_map/rd,rf->df/dot_general | solution.py:97
  270.5 9.0 %convolution_convert_fusion = bf16[2048,1536]{0,1:T(8,128)(2,1)} fusion(bf16[2048,768]{1,0:T(8,128)(2,1)} %copy-done.4, bf16[1536,768]{1,0:T(8,128)(2,1)S(1)} %copy-done), kind=kOutput, calls=%fused_computation.22 | convolution fusion | flops 4834983936 | bytes 11796480 | tf_op jit(solution)/shard_map/rf,df->rd/dot_general | solution.py:104
  282.6 9.6 %subtract_multiply_fusion = f32[2048,1536]{0,1:T(8,128)} fusion(bf16[2048,1536]{0,1:T(8,128)(2,1)} %copy.13, f32[2048]{0:T(1024)S(1)} %add_rsqrt_fusion, f32[2048]{0:T(1024)S(1)} %broadcast_multiply_fusion.1), kind=kLoop, calls=%fused_computation.16 | loop fusion | flops 9437184 | bytes 18890752 | tf_op jit(solution)/shard_map/mul | solution.py:23
  292.1 54.4 %reduce-scatter.6.cloned.1.call-done = f32[96,768]{1,0:T(8,128)} async-done(((f32[1536,768]{1,0:T(8,128)}), f32[96,768]{1,0:T(8,128)}) %reduce-scatter.6.cloned.1.call-update) | async-done | bytes 294928 | tf_op jit(solution)/shard_map/reduce_scatter | solution.py:99
  348.2 84.6 %reduce-scatter.8.cloned.1.call-done = f32[768,96]{0,1:T(8,128)} async-done(((f32[768,1536]{0,1:T(8,128)}), f32[768,96]{0,1:T(8,128)}) %reduce-scatter.8.cloned.1.call-update) | async-done | bytes 294928 | tf_op jit(solution)/shard_map/reduce_scatter | solution.py:100
  434.4 129.8 %reduce-scatter.4.cloned.1.call-done = bf16[2048,192]{0,1:T(8,128)(2,1)} async-done(((bf16[2048,1536]{0,1:T(8,128)(2,1)}), bf16[2048,192]{0,1:T(8,128)(2,1)}) %reduce-scatter.4.cloned.1.call-update) | async-done | bytes 786448 | tf_op jit(solution)/shard_map/reduce_scatter | solution.py:105
  566.1 32.6 %all-reduce = (f32[2048]{0:T(1024)S(1)}, f32[2048]{0:T(1024)S(1)}) all-reduce(f32[2048]{0:T(1024)S(1)} %get-tuple-element.259, f32[2048]{0:T(1024)S(1)} %get-tuple-element.258), channel_id=1, replica_groups=mesh['dp'=16,'tensor'=8] {'tensor'}, use_global_device_ids=true, to_apply=%region_14.15 | all-reduce | flops 4096 | bytes 32768 | tf_op jit(solution)/shard_map/psum | solution.py:109
  (188 shorter events, 144.5 us)
Async XLA Ops:
  7.2 339.4 %reduce-scatter.6.cloned.1.call-start = ((), (), s32[]{:S(2)}) async-start(), calls=%async_computation.4 | async-start | bytes 5013504 | tf_op jit(solution)/shard_map/reduce_scatter | solution.py:99
  99.2 6.9 %collective-permute-start = (bf16[8,1536]{1,0:T(8,128)(2,1)S(1)}, bf16[8,1536]{1,0:T(8,128)(2,1)S(1)}, u32[]{:S(2)}, u32[]{:S(2)}) collective-permute-start(bf16[8,1536]{1,0:T(8,128)(2,1)S(1)} %copy.24), channel_id=1, source_target_pairs={{120,0},{0,8},{8,16},{16,24},{24,32},{32,40},{40,48},{48,56},{56,6... | collective-permute-start | bytes 73736 | tf_op jit(solution)/shard_map/while/body/eval_jaxpr/ppermute | solution.py:16
  101.6 7.1 %collective-permute-start.1 = (f32[8,1536]{1,0:T(8,128)S(1)}, f32[8,1536]{1,0:T(8,128)S(1)}, u32[]{:S(2)}, u32[]{:S(2)}) collective-permute-start(f32[8,1536]{1,0:T(8,128)S(1)} %fusion.71), channel_id=1, source_target_pairs={{120,0},{0,8},{8,16},{16,24},{24,32},{32,40},{40,48},{48,56},{56,6... | collective-permute-start | bytes 147464 | tf_op jit(solution)/shard_map/while/body/eval_jaxpr/ppermute | solution.py:16
  108.7 6.9 %collective-permute-start = (bf16[8,1536]{1,0:T(8,128)(2,1)S(1)}, bf16[8,1536]{1,0:T(8,128)(2,1)S(1)}, u32[]{:S(2)}, u32[]{:S(2)}) collective-permute-start(bf16[8,1536]{1,0:T(8,128)(2,1)S(1)} %copy.24), channel_id=1, source_target_pairs={{120,0},{0,8},{8,16},{16,24},{24,32},{32,40},{40,48},{48,56},{56,6... | collective-permute-start | bytes 73736 | tf_op jit(solution)/shard_map/while/body/eval_jaxpr/ppermute | solution.py:16
  111.0 7.1 %collective-permute-start.1 = (f32[8,1536]{1,0:T(8,128)S(1)}, f32[8,1536]{1,0:T(8,128)S(1)}, u32[]{:S(2)}, u32[]{:S(2)}) collective-permute-start(f32[8,1536]{1,0:T(8,128)S(1)} %fusion.71), channel_id=1, source_target_pairs={{120,0},{0,8},{8,16},{16,24},{24,32},{32,40},{40,48},{48,56},{56,6... | collective-permute-start | bytes 147464 | tf_op jit(solution)/shard_map/while/body/eval_jaxpr/ppermute | solution.py:16
  120.4 7.1 %collective-permute-start.1 = (f32[8,1536]{1,0:T(8,128)S(1)}, f32[8,1536]{1,0:T(8,128)S(1)}, u32[]{:S(2)}, u32[]{:S(2)}) collective-permute-start(f32[8,1536]{1,0:T(8,128)S(1)} %fusion.71), channel_id=1, source_target_pairs={{120,0},{0,8},{8,16},{16,24},{24,32},{32,40},{40,48},{48,56},{56,6... | collective-permute-start | bytes 147464 | tf_op jit(solution)/shard_map/while/body/eval_jaxpr/ppermute | solution.py:16
  129.8 7.1 %collective-permute-start.1 = (f32[8,1536]{1,0:T(8,128)S(1)}, f32[8,1536]{1,0:T(8,128)S(1)}, u32[]{:S(2)}, u32[]{:S(2)}) collective-permute-start(f32[8,1536]{1,0:T(8,128)S(1)} %fusion.71), channel_id=1, source_target_pairs={{120,0},{0,8},{8,16},{16,24},{24,32},{32,40},{40,48},{48,56},{56,6... | collective-permute-start | bytes 147464 | tf_op jit(solution)/shard_map/while/body/eval_jaxpr/ppermute | solution.py:16
  136.9 6.9 %collective-permute-start = (bf16[8,1536]{1,0:T(8,128)(2,1)S(1)}, bf16[8,1536]{1,0:T(8,128)(2,1)S(1)}, u32[]{:S(2)}, u32[]{:S(2)}) collective-permute-start(bf16[8,1536]{1,0:T(8,128)(2,1)S(1)} %copy.24), channel_id=1, source_target_pairs={{120,0},{0,8},{8,16},{16,24},{24,32},{32,40},{40,48},{48,56},{56,6... | collective-permute-start | bytes 73736 | tf_op jit(solution)/shard_map/while/body/eval_jaxpr/ppermute | solution.py:16
  139.2 7.1 %collective-permute-start.1 = (f32[8,1536]{1,0:T(8,128)S(1)}, f32[8,1536]{1,0:T(8,128)S(1)}, u32[]{:S(2)}, u32[]{:S(2)}) collective-permute-start(f32[8,1536]{1,0:T(8,128)S(1)} %fusion.71), channel_id=1, source_target_pairs={{120,0},{0,8},{8,16},{16,24},{24,32},{32,40},{40,48},{48,56},{56,6... | collective-permute-start | bytes 147464 | tf_op jit(solution)/shard_map/while/body/eval_jaxpr/ppermute | solution.py:16
  146.4 6.9 %collective-permute-start = (bf16[8,1536]{1,0:T(8,128)(2,1)S(1)}, bf16[8,1536]{1,0:T(8,128)(2,1)S(1)}, u32[]{:S(2)}, u32[]{:S(2)}) collective-permute-start(bf16[8,1536]{1,0:T(8,128)(2,1)S(1)} %copy.24), channel_id=1, source_target_pairs={{120,0},{0,8},{8,16},{16,24},{24,32},{32,40},{40,48},{48,56},{56,6... | collective-permute-start | bytes 73736 | tf_op jit(solution)/shard_map/while/body/eval_jaxpr/ppermute | solution.py:16
  148.7 7.1 %collective-permute-start.1 = (f32[8,1536]{1,0:T(8,128)S(1)}, f32[8,1536]{1,0:T(8,128)S(1)}, u32[]{:S(2)}, u32[]{:S(2)}) collective-permute-start(f32[8,1536]{1,0:T(8,128)S(1)} %fusion.71), channel_id=1, source_target_pairs={{120,0},{0,8},{8,16},{16,24},{24,32},{32,40},{40,48},{48,56},{56,6... | collective-permute-start | bytes 147464 | tf_op jit(solution)/shard_map/while/body/eval_jaxpr/ppermute | solution.py:16
  158.1 7.1 %collective-permute-start.1 = (f32[8,1536]{1,0:T(8,128)S(1)}, f32[8,1536]{1,0:T(8,128)S(1)}, u32[]{:S(2)}, u32[]{:S(2)}) collective-permute-start(f32[8,1536]{1,0:T(8,128)S(1)} %fusion.71), channel_id=1, source_target_pairs={{120,0},{0,8},{8,16},{16,24},{24,32},{32,40},{40,48},{48,56},{56,6... | collective-permute-start | bytes 147464 | tf_op jit(solution)/shard_map/while/body/eval_jaxpr/ppermute | solution.py:16
  167.5 7.1 %collective-permute-start.1 = (f32[8,1536]{1,0:T(8,128)S(1)}, f32[8,1536]{1,0:T(8,128)S(1)}, u32[]{:S(2)}, u32[]{:S(2)}) collective-permute-start(f32[8,1536]{1,0:T(8,128)S(1)} %fusion.71), channel_id=1, source_target_pairs={{120,0},{0,8},{8,16},{16,24},{24,32},{32,40},{40,48},{48,56},{56,6... | collective-permute-start | bytes 147464 | tf_op jit(solution)/shard_map/while/body/eval_jaxpr/ppermute | solution.py:16
  174.6 6.9 %collective-permute-start = (bf16[8,1536]{1,0:T(8,128)(2,1)S(1)}, bf16[8,1536]{1,0:T(8,128)(2,1)S(1)}, u32[]{:S(2)}, u32[]{:S(2)}) collective-permute-start(bf16[8,1536]{1,0:T(8,128)(2,1)S(1)} %copy.24), channel_id=1, source_target_pairs={{120,0},{0,8},{8,16},{16,24},{24,32},{32,40},{40,48},{48,56},{56,6... | collective-permute-start | bytes 73736 | tf_op jit(solution)/shard_map/while/body/eval_jaxpr/ppermute | solution.py:16
  176.9 7.1 %collective-permute-start.1 = (f32[8,1536]{1,0:T(8,128)S(1)}, f32[8,1536]{1,0:T(8,128)S(1)}, u32[]{:S(2)}, u32[]{:S(2)}) collective-permute-start(f32[8,1536]{1,0:T(8,128)S(1)} %fusion.71), channel_id=1, source_target_pairs={{120,0},{0,8},{8,16},{16,24},{24,32},{32,40},{40,48},{48,56},{56,6... | collective-permute-start | bytes 147464 | tf_op jit(solution)/shard_map/while/body/eval_jaxpr/ppermute | solution.py:16
  186.3 7.1 %collective-permute-start.1 = (f32[8,1536]{1,0:T(8,128)S(1)}, f32[8,1536]{1,0:T(8,128)S(1)}, u32[]{:S(2)}, u32[]{:S(2)}) collective-permute-start(f32[8,1536]{1,0:T(8,128)S(1)} %fusion.71), channel_id=1, source_target_pairs={{120,0},{0,8},{8,16},{16,24},{24,32},{32,40},{40,48},{48,56},{56,6... | collective-permute-start | bytes 147464 | tf_op jit(solution)/shard_map/while/body/eval_jaxpr/ppermute | solution.py:16
  195.7 7.1 %collective-permute-start.1 = (f32[8,1536]{1,0:T(8,128)S(1)}, f32[8,1536]{1,0:T(8,128)S(1)}, u32[]{:S(2)}, u32[]{:S(2)}) collective-permute-start(f32[8,1536]{1,0:T(8,128)S(1)} %fusion.71), channel_id=1, source_target_pairs={{120,0},{0,8},{8,16},{16,24},{24,32},{32,40},{40,48},{48,56},{56,6... | collective-permute-start | bytes 147464 | tf_op jit(solution)/shard_map/while/body/eval_jaxpr/ppermute | solution.py:16
  205.2 7.1 %collective-permute-start.1 = (f32[8,1536]{1,0:T(8,128)S(1)}, f32[8,1536]{1,0:T(8,128)S(1)}, u32[]{:S(2)}, u32[]{:S(2)}) collective-permute-start(f32[8,1536]{1,0:T(8,128)S(1)} %fusion.71), channel_id=1, source_target_pairs={{120,0},{0,8},{8,16},{16,24},{24,32},{32,40},{40,48},{48,56},{56,6... | collective-permute-start | bytes 147464 | tf_op jit(solution)/shard_map/while/body/eval_jaxpr/ppermute | solution.py:16
  214.6 7.1 %collective-permute-start.1 = (f32[8,1536]{1,0:T(8,128)S(1)}, f32[8,1536]{1,0:T(8,128)S(1)}, u32[]{:S(2)}, u32[]{:S(2)}) collective-permute-start(f32[8,1536]{1,0:T(8,128)S(1)} %fusion.71), channel_id=1, source_target_pairs={{120,0},{0,8},{8,16},{16,24},{24,32},{32,40},{40,48},{48,56},{56,6... | collective-permute-start | bytes 147464 | tf_op jit(solution)/shard_map/while/body/eval_jaxpr/ppermute | solution.py:16
  224.0 7.1 %collective-permute-start.1 = (f32[8,1536]{1,0:T(8,128)S(1)}, f32[8,1536]{1,0:T(8,128)S(1)}, u32[]{:S(2)}, u32[]{:S(2)}) collective-permute-start(f32[8,1536]{1,0:T(8,128)S(1)} %fusion.71), channel_id=1, source_target_pairs={{120,0},{0,8},{8,16},{16,24},{24,32},{32,40},{40,48},{48,56},{56,6... | collective-permute-start | bytes 147464 | tf_op jit(solution)/shard_map/while/body/eval_jaxpr/ppermute | solution.py:16
  233.4 7.1 %collective-permute-start.1 = (f32[8,1536]{1,0:T(8,128)S(1)}, f32[8,1536]{1,0:T(8,128)S(1)}, u32[]{:S(2)}, u32[]{:S(2)}) collective-permute-start(f32[8,1536]{1,0:T(8,128)S(1)} %fusion.71), channel_id=1, source_target_pairs={{120,0},{0,8},{8,16},{16,24},{24,32},{32,40},{40,48},{48,56},{56,6... | collective-permute-start | bytes 147464 | tf_op jit(solution)/shard_map/while/body/eval_jaxpr/ppermute | solution.py:16
  242.8 7.1 %collective-permute-start.1 = (f32[8,1536]{1,0:T(8,128)S(1)}, f32[8,1536]{1,0:T(8,128)S(1)}, u32[]{:S(2)}, u32[]{:S(2)}) collective-permute-start(f32[8,1536]{1,0:T(8,128)S(1)} %fusion.71), channel_id=1, source_target_pairs={{120,0},{0,8},{8,16},{16,24},{24,32},{32,40},{40,48},{48,56},{56,6... | collective-permute-start | bytes 147464 | tf_op jit(solution)/shard_map/while/body/eval_jaxpr/ppermute | solution.py:16
  267.4 165.4 %reduce-scatter.8.cloned.1.call-start = ((), (), s32[]{:S(2)}) async-start(), calls=%async_computation.5 | async-start | bytes 5013504 | tf_op jit(solution)/shard_map/reduce_scatter | solution.py:100
  270.4 293.8 %reduce-scatter.4.cloned.1.call-start = ((), (), s32[]{:S(2)}) async-start(), calls=%async_computation.3 | async-start | bytes 7077888 | tf_op jit(solution)/shard_map/reduce_scatter | solution.py:105
  (20 other events, 151.7 us)
Sparse Core Ops, SparseCore 0:
  267.5 78.9 reduce-scatter.5
  351.1 81.5 reduce-scatter.7
  435.2 128.9 reduce-scatter.3
where the time goes:
time: 610 us; the launch traced here: 609 us
  waiting for transfers between devices  369 us (60%)
  matrix products  79 us (13%)
  blocking collectives  69 us (11%)
  other arithmetic  47.2 us (8%)
  local copies, waits for them, and re-layouts  28.7 us (5%)
  between operations  13.9 us (2%)
    reduce_scatter x1, waiting for transfers between devices, body(): lax.psum_scatter(partial_feats.astype(jnp.bfloat16), 'tensor', scatter_di...  130 us
    ppermute x32, waiting for transfers between devices, shifted(): return lax.ppermute(block, axis, route)  99.8 us
    reduce_scatter x1, waiting for transfers between devices, body(): lax.psum_scatter(w_out_part, 'dp', scatter_dimension=1, tiled=True)  84.6 us
    reduce_scatter x1, waiting for transfers between devices, body(): lax.psum_scatter(w_in_part, 'dp', scatter_dimension=0, tiled=True)  54.4 us
    psum x1, blocking collectives, body(): lax.psum(jnp.dot(pooled_bf, w_out, preferred_element_type=jnp.float32), '...  36.4 us
    psum x1, blocking collectives, body(): lax.psum((jnp.sum(summed, axis=1), jnp.sum(summed * normed_cols, axis=1))...  32.6 us
    unnamed x21, local copies, waits for them, and re-layouts  28.1 us
    dot_general x16, matrix products, sig_grads(): jnp.dot(image_bf, text_bf.T, preferred_element_type=jnp.float32)  22.8 us
  transfers between devices with their start and end apart: 35, of which 35 were waited for; matrix products, arithmetic and copies ran while one was open for 13% of the time, Pallas kernels for 0%

commit v1 on v0

v1 whole, which is shorter than its diff:
```python
import math

import jax
import jax.numpy as jnp
from jax import lax
from jax.experimental import pallas as pl
from jax.experimental.pallas import tpu as pltpu
from jax.sharding import PartitionSpec as P

F32 = jnp.float32
BF16 = jnp.bfloat16

D = 1536
HALF = D // 2
HID = 768
ROWS = 2048
TOKS = 256
IMGS = 8
LOSS_SCALE = 64.0
EPS = 1e-06
GELU_A = math.sqrt(2.0 / math.pi)
GELU_B = 0.044715

PAIR_FIRST = 3
CHUNKS = 8

NN = (((1,), (0,)), ((), ()))
NT = (((1,), (1,)), ((), ()))
TN = (((0,), (0,)), ((), ()))


def dot(a, b, dims=NN):
    return lax.dot_general(a, b, dims, preferred_element_type=F32)


def kernel(
    tokens_hbm, w_in_hbm, w_out_hbm, text_ref, labels_ref, scale_ref, bias_ref,
    out_ref, win_ref, wout_ref, tgrad_ref,
    tok, inv, hpre, hg, nt, w_in, w_out,
    tmean, pooled, pgs, egs, ones_cs, part, part2, tdir,
    texts, ebuf, msgs,
    q, ra, rb, sa, sb, yr, yq,
    g, gc, gx, gra, grb, gsa, gsb, gyr,
    tok_sem, w_sem,
    text_ss, text_rs, emb_ss, emb_rs, msg_ss, msg_rs,
    q_ss, q_rs, g_ss, g_rs,
):
    dp = lax.axis_index("dp")
    tp = lax.axis_index("tensor")
    yh, local = dp // 8, dp % 8
    x, core = local // 2, dp % 2
    z, y = tp // 2, tp % 2

    def mesh_z(step):
        return (dp, ((z + step) % 4) * 2 + y)

    def mesh_x(step):
        return (yh * 8 + ((x + step) % 4) * 2 + core, tp)

    y_pair = (dp, z * 2 + (1 - y))
    core_pair = (dp - core + (1 - core), tp)
    y_far = ((1 - yh) * 8 + local, tp)

    def octet(k):
        return (yh * 8 + (local + k) % 8, tp)

    def remote(src, dst, ssem, rsem, dev):
        return pltpu.make_async_remote_copy(
            src_ref=src, dst_ref=dst, send_sem=ssem, recv_sem=rsem,
            device_id=dev, device_id_type=pl.DeviceIdType.MESH,
        )

    def tok_copy(c):
        rows = pl.ds(c * TOKS, TOKS)
        return pltpu.make_async_copy(tokens_hbm.at[rows], tok.at[rows], tok_sem.at[c])

    tok_copy(0).start()
    w_in_copy = pltpu.make_async_copy(w_in_hbm, w_in, w_sem.at[0])
    w_out_copy = pltpu.make_async_copy(w_out_hbm, w_out, w_sem.at[1])
    w_in_copy.start()

    @pl.loop(1, CHUNKS)
    def _(c):
        tok_copy(c).start()

    w_out_copy.start()

    barrier = pltpu.get_barrier_semaphore()

    def greet(dev):
        pl.semaphore_signal(barrier, inc=1, device_id=dev, device_id_type=pl.DeviceIdType.MESH)

    greet(y_far)
    for k in range(1, 8):
        greet(octet(k))
        greet((dp, (tp + k) % 8))

    text_vals = text_ref[...].astype(F32)
    text_inv = lax.rsqrt(jnp.sum(text_vals * text_vals, axis=1, keepdims=True) + EPS)
    text_nrm = text_vals * text_inv
    texts[dp] = jnp.concatenate([text_nrm[:, :HALF], text_nrm[:, HALF:]], axis=0).astype(BF16)

    pl.semaphore_wait(barrier, 15)

    def gather_send(buf, slot, ss, rs, row):
        @pl.loop(1, 8)
        def _(k):
            remote(buf.at[slot], buf.at[slot], ss.at[row, k], rs.at[slot], octet(k)).start()

    def gather_far(buf, ss, rs):
        return remote(buf.at[dp], buf.at[dp], ss.at[0, 0], rs.at[dp], y_far)

    def gather_recv(buf, slot, ss, rs):
        remote(buf.at[slot], buf.at[slot], ss.at[0, 0], rs.at[slot], y_far).wait_recv()

    def gather_first(buf, ss, rs):
        gather_far(buf, ss, rs).start()
        gather_send(buf, dp, ss, rs, 0)

    far_slot = (1 - yh) * 8 + local

    def gather_relay(buf, ss, rs):
        gather_recv(buf, far_slot, ss, rs)
        gather_send(buf, far_slot, ss, rs, 1)

    def gather_rest(buf, ss, rs):
        @pl.loop(1, 8)
        def _(k):
            gather_recv(buf, yh * 8 + (local + k) % 8, ss, rs)
            gather_recv(buf, (1 - yh) * 8 + (local + k) % 8, ss, rs)

    def gather_sent(buf, ss, rs):
        gather_far(buf, ss, rs).wait_send()

        @pl.loop(1, 8)
        def _(k):
            for row in range(2):
                remote(buf.at[dp], buf.at[dp], ss.at[row, k], rs.at[dp], octet(k)).wait_send()

    gather_first(texts, text_ss, text_rs)

    w_in_copy.wait()

    @pl.loop(0, CHUNKS)
    def _(c):
        tok_copy(c).wait()

        def norm_rows(b, acc):
            rows = pl.ds(pl.multiple_of(c * TOKS + b * 32, 32), 32)
            vals = tok[rows, :].astype(F32)
            mean = jnp.sum(vals, axis=1, keepdims=True) * (1.0 / D)
            center = vals - mean
            var = jnp.sum(center * center, axis=1, keepdims=True) * (1.0 / D)
            scale = lax.rsqrt(var + EPS)
            tok[rows, :] = (center * scale).astype(BF16)
            inv[rows, :] = scale
            return acc + jnp.sum(vals.reshape(4, 8, D), axis=0)

        acc = lax.fori_loop(0, 8, norm_rows, jnp.zeros((8, D), F32))
        tmean[pl.ds(c, 1), :] = jnp.sum(acc, axis=0, keepdims=True) * (1.0 / TOKS)
        rows = pl.ds(pl.multiple_of(c * TOKS, TOKS), TOKS)
        hpre[rows, :] = dot(tok[rows, :], w_in[...])

        def pool_rows(b, acc):
            h = hpre[pl.ds(pl.multiple_of(c * TOKS + b * 32, 32), 32), :]
            t = jnp.tanh(GELU_A * (h + GELU_B * (h * h * h)))
            return acc + jnp.sum((0.5 * h * (1.0 + t)).reshape(4, 8, HID), axis=0)

        acc = lax.fori_loop(0, 8, pool_rows, jnp.zeros((8, HID), F32))
        pooled[pl.ds(c, 1), :] = jnp.sum(acc, axis=0, keepdims=True) * (1.0 / TOKS)

    w_out_copy.wait()
    pooled_bf = pooled[...].astype(BF16)
    part_emb = dot(pooled_bf, w_out[...])
    ebuf[tp] = jnp.concatenate([part_emb[:, :HALF], part_emb[:, HALF:]], axis=0).astype(BF16)

    def emb_copy(k):
        return remote(ebuf.at[tp], ebuf.at[tp], emb_ss.at[k], emb_rs.at[tp], (dp, (tp + k) % 8))

    @pl.loop(1, 8)
    def _(k):
        emb_copy(k).start()

    gather_relay(texts, text_ss, text_rs)

    @pl.loop(0, CHUNKS)
    def _(c):
        rows = pl.ds(pl.multiple_of(c * TOKS, TOKS), TOKS)
        nt[:, rows] = tok[rows, :].T

    def col_sum(b, acc):
        vals = w_in[pl.ds(pl.multiple_of(b * 32, 32), 32), :].astype(F32)
        return acc + jnp.sum(vals.reshape(4, 8, HID), axis=0)

    acc = lax.fori_loop(0, D // 32, col_sum, jnp.zeros((8, HID), F32))
    ones_cs[...] = jnp.sum(acc, axis=0, keepdims=True) * (1.0 / D)

    @pl.loop(1, 8)
    def _(k):
        src = (tp + k) % 8
        remote(ebuf.at[src], ebuf.at[src], emb_ss.at[k], emb_rs.at[src], (dp, src)).wait_recv()

    tm = tmean[...]
    emb = jnp.concatenate([tm[:, :HALF], tm[:, HALF:]], axis=0)
    for k in range(8):
        emb = emb + ebuf[k].astype(F32)

    def both(sums):
        total = sums[:IMGS] + sums[IMGS:]
        return jnp.concatenate([total, total], axis=0)

    emb_inv = lax.rsqrt(both(jnp.sum(emb * emb, axis=1, keepdims=True)) + EPS)
    image_bf = (emb * emb_inv).astype(BF16)

    gather_rest(texts, text_ss, text_rs)
    text_all = texts[...].reshape(256, HALF)
    prod = dot(image_bf, text_all, NT)
    scale = scale_ref[0]
    logits = scale * (prod[:IMGS] + pltpu.roll(prod[IMGS:], 256 - IMGS, 1)) + bias_ref[0]
    lane = lax.broadcasted_iota(jnp.int32, (IMGS, 256), 1)
    row = lax.broadcasted_iota(jnp.int32, (IMGS, 256), 0)
    valid = (lane % 16) < 8
    text_id = (lane // 16) * 8 + lane % 16
    label = jnp.zeros((IMGS, 256), jnp.int32)
    for k in range(IMGS):
        label = jnp.where(row == k, labels_ref[k], label)
    signs = jnp.where(label == text_id, 1.0, -1.0)
    grad = -signs * jax.nn.sigmoid(-signs * logits) * LOSS_SCALE
    grad = jnp.where(valid, grad, 0.0)
    grad = jnp.concatenate([grad, pltpu.roll(grad, IMGS, 1)], axis=0).astype(BF16)
    image_dir = scale * dot(grad, text_all)
    emb_grad = emb_inv * image_dir - (emb_inv * emb_inv * emb_inv) * emb * both(
        jnp.sum(emb * image_dir, axis=1, keepdims=True)
    )
    egs[...] = emb_grad * (1.0 / TOKS)
    eg_bf = emb_grad.astype(BF16)
    pgs[...] = (
        dot(eg_bf[:IMGS], w_out[:, :HALF], NT) + dot(eg_bf[IMGS:], w_out[:, HALF:], NT)
    ) * (1.0 / TOKS)

    msgs[dp, :, 0:HALF] = image_bf
    msgs[dp, :, HALF:D] = eg_bf
    pooled_f = pooled[...]
    msgs[dp, :, D:D + HID] = jnp.concatenate([pooled_f, pooled_f], axis=0).astype(BF16)
    msgs[dp, :, D + HID:D + HID + 256] = grad

    def hidden_chunk(c):
        pg = pgs[pl.ds(c, 1), :]
        cs = ones_cs[...]

        @pl.loop(0, 8)
        def _(b):
            rows = pl.ds(pl.multiple_of(c * TOKS + b * 32, 32), 32)
            h = hpre[rows, :]
            h2 = h * h
            t = jnp.tanh(GELU_A * (h + GELU_B * (h2 * h)))
            slope = 0.5 * (1.0 + t) + (0.5 * GELU_A) * h * (1.0 - t * t) * (
                1.0 + (3.0 * GELU_B) * h2
            )
            grad_bf = (slope * pg).astype(BF16)
            hg[rows, :] = grad_bf
            grad_h = grad_bf.astype(F32)
            p1 = grad_h * cs
            p2 = grad_h * h
            s1 = p1[:, 0:128]
            s2 = p2[:, 0:128]
            for i in range(1, HID // 128):
                s1 = s1 + p1[:, i * 128:(i + 1) * 128]
                s2 = s2 + p2[:, i * 128:(i + 1) * 128]
            own = pl.ds(pl.multiple_of(b * 32, 32), 32)
            part[own, :] = s1
            part2[own, :] = s2

        m1 = jnp.sum(part[...].T, axis=0, keepdims=True)
        m2 = jnp.sum(part2[...].T, axis=0, keepdims=True) * (1.0 / D)
        rows = pl.ds(pl.multiple_of(c * TOKS, TOKS), TOKS)
        hgc = hg[rows, :]

        @pl.loop(0, 4)
        def _(zb):
            feats = pl.ds(pl.multiple_of(zb * 384, 384), 384)
            block = dot(w_in[feats, :], hgc, NT) - m1 - nt[feats, rows].astype(F32) * m2
            block = block.astype(BF16)
            q[c, zb, 0] = block[:192]
            q[c, zb, 1] = block[192:]

    zp, zn, zo = (z + 1) % 4, (z + 3) % 4, (z + 2) % 4
    up, down = mesh_z(1), mesh_z(3)
    lo, hi = pl.ds(0, 96), pl.ds(96, 96)

    def pair_copy(c):
        return remote(q.at[c, :, 1 - y], yq.at[c], q_ss.at[c, 0], q_rs.at[c, 0], y_pair)

    def pair_ring1(c):
        return (
            remote(q.at[c, zo, y, lo], ra.at[c, lo], q_ss.at[c, 1], q_rs.at[c, 1], up),
            remote(q.at[c, zo, y, hi], rb.at[c, lo], q_ss.at[c, 2], q_rs.at[c, 2], down),
            remote(q.at[c, zp, y, hi], sa.at[c, 0, hi], q_ss.at[c, 3], q_rs.at[c, 3], up),
            remote(q.at[c, zn, y, lo], sb.at[c, 0, lo], q_ss.at[c, 4], q_rs.at[c, 4], down),
        )

    def pair_ring2(c):
        return (
            remote(q.at[c, zp, y, lo], sa.at[c, 0, lo], q_ss.at[c, 5], q_rs.at[c, 5], up),
            remote(q.at[c, zn, y, hi], sb.at[c, 0, hi], q_ss.at[c, 6], q_rs.at[c, 6], down),
        )

    def ring1(c):
        return (
            remote(q.at[c, zo, 0], ra.at[c], q_ss.at[c, 1], q_rs.at[c, 1], up),
            remote(q.at[c, zo, 1], rb.at[c], q_ss.at[c, 2], q_rs.at[c, 2], down),
            remote(q.at[c, zp, 1], sa.at[c, 1], q_ss.at[c, 3], q_rs.at[c, 3], up),
            remote(q.at[c, zn, 0], sb.at[c, 0], q_ss.at[c, 4], q_rs.at[c, 4], down),
        )

    def ring2(c):
        return (
            remote(q.at[c, zp, 0], sa.at[c, 0], q_ss.at[c, 5], q_rs.at[c, 5], up),
            remote(q.at[c, zn, 1], sb.at[c, 1], q_ss.at[c, 6], q_rs.at[c, 6], down),
        )

    def ring_pair(c):
        return remote(q.at[c, z, 1 - y], yr.at[c], q_ss.at[c, 0], q_rs.at[c, 0], y_pair)

    @pl.loop(0, PAIR_FIRST)
    def _(c):
        hidden_chunk(c)
        pair_copy(c).start()

    @pl.loop(PAIR_FIRST, CHUNKS)
    def _(c):
        hidden_chunk(c)
        for copy in ring1(c):
            copy.start()

    gather_first(msgs, msg_ss, msg_rs)

    @pl.loop(0, 4)
    def _(i):
        feats = pl.ds(pl.multiple_of(i * 384, 384), 384)
        block = dot(nt[feats, :], hg[...]).astype(BF16)
        for k in range(4):
            g[i, k // 2, k % 2] = block[k * 96:(k + 1) * 96]

    core_copy = remote(g.at[:, :, 1 - core], gc, g_ss.at[0], g_rs.at[0], core_pair)
    core_copy.start()

    def add_into(dst, a, b):
        dst[...] = (a[...].astype(F32) + b[...].astype(F32)).astype(BF16)

    @pl.loop(0, PAIR_FIRST)
    def _(c):
        pair_copy(c).wait_recv()
        for zb in range(4):
            blk = q.at[c, zb, y]
            add_into(blk, blk, yq.at[c, zb])
        for copy in pair_ring1(c):
            copy.start()

    core_copy.wait_recv()

    @pl.loop(0, 8)
    def _(k):
        xb, yb = k // 2, k % 2
        i, j = yb * 2 + xb // 2, xb % 2
        add_into(gx.at[xb, yb], g.at[i, j, core], gc.at[i, j])

    xp, xn, xo = (x + 1) % 4, (x + 3) % 4, (x + 2) % 4
    right, left = mesh_x(1), mesh_x(3)
    g1a = remote(gx.at[xo, 0], gra, g_ss.at[1], g_rs.at[1], right)
    g1b = remote(gx.at[xo, 1], grb, g_ss.at[2], g_rs.at[2], left)
    g2a = remote(gx.at[xp], gsa, g_ss.at[3], g_rs.at[3], right)
    g2b = remote(gx.at[xn], gsb, g_ss.at[4], g_rs.at[4], left)
    g3 = remote(gx.at[x, 1 - yh], gyr, g_ss.at[5], g_rs.at[5], y_far)
    g1a.start()
    g1b.start()

    gather_relay(msgs, msg_ss, msg_rs)

    @pl.loop(PAIR_FIRST, CHUNKS)
    def _(c):
        first, second = ring1(c)[:2]
        first.wait_recv()
        blk = q.at[c, zp, 0]
        add_into(blk, blk, ra.at[c])
        second.wait_recv()
        blk = q.at[c, zn, 1]
        add_into(blk, blk, rb.at[c])
        for copy in ring2(c):
            copy.start()

    g1a.wait_recv()
    add_into(gx.at[xp, 0], gx.at[xp, 0], gra)
    g1b.wait_recv()
    add_into(gx.at[xn, 1], gx.at[xn, 1], grb)
    g2a.start()
    g2b.start()

    @pl.loop(0, PAIR_FIRST)
    def _(c):
        first, second = pair_ring1(c)[:2]
        first.wait_recv()
        blk = q.at[c, zp, y, lo]
        add_into(blk, blk, ra.at[c, lo])
        second.wait_recv()
        blk = q.at[c, zn, y, hi]
        add_into(blk, blk, rb.at[c, lo])
        for copy in pair_ring2(c):
            copy.start()

    gather_rest(msgs, msg_ss, msg_rs)
    all_msgs = msgs[...].reshape(256, D + HID + 256)
    tdir[...] = dot(all_msgs[:, D + HID:], all_msgs[:, :HALF], TN)
    text_dir = scale * tdir[pl.ds(pl.multiple_of(dp * 16, 16), 16), :]
    text_dir = jnp.concatenate([text_dir[:IMGS], text_dir[IMGS:]], axis=1)
    tgrad_ref[...] = (
        text_inv * text_dir
        - (text_inv * text_inv * text_inv) * text_vals
        * jnp.sum(text_vals * text_dir, axis=1, keepdims=True)
    ).astype(BF16)
    feat = lax.broadcasted_iota(jnp.int32, (HALF, 128), 0)
    col = lax.broadcasted_iota(jnp.int32, (HALF, 128), 1)
    pick = jnp.where(feat == col + local * 96, 1.0, 0.0).astype(BF16)
    emb_cols = dot(all_msgs[:, HALF:D], pick)
    slot_row = lax.broadcasted_iota(jnp.int32, (256, 128), 0)
    emb_cols = jnp.where((slot_row // 8) % 2 == yh, emb_cols, 0.0).astype(BF16)
    wout_ref[...] = dot(all_msgs[:, D:D + HID], emb_cols, TN)[:, :96].astype(BF16)

    @pl.loop(PAIR_FIRST, CHUNKS)
    def _(c):
        for copy in ring1(c)[2:] + ring2(c):
            copy.wait_recv()
        for half in range(2):
            blk = q.at[c, z, half]
            blk[...] = (
                blk[...].astype(F32) + sa[c, half].astype(F32) + sb[c, half].astype(F32)
            ).astype(BF16)
        ring_pair(c).start()

    g2a.wait_recv()
    g2b.wait_recv()
    for half in range(2):
        blk = gx.at[x, half]
        blk[...] = (
            blk[...].astype(F32) + gsa[half].astype(F32) + gsb[half].astype(F32)
        ).astype(BF16)
    g3.start()

    eg_cols = egs[pl.ds(pl.multiple_of((z // 2) * 8, 8), 8),
                  pl.ds(pl.multiple_of((z % 2) * 384, 128), 384)]
    eg_cols = jnp.where(y == 0, eg_cols[:, :192], eg_cols[:, 192:])
    tdir[0:8, 0:192] = eg_cols

    def finish(c, total):
        rows = pl.ds(pl.multiple_of(c * TOKS, TOKS), TOKS)
        square = jnp.concatenate([total, jnp.zeros((64, 256), F32)], axis=0).T
        out_ref[rows, :] = (
            inv[rows, :] * square[:, :192] + tdir[pl.ds(c, 1), 0:192]
        ).astype(BF16)

    @pl.loop(0, PAIR_FIRST)
    def _(c):
        for copy in pair_ring1(c)[2:] + pair_ring2(c):
            copy.wait_recv()
        finish(c, q[c, z, y].astype(F32) + sa[c, 0].astype(F32) + sb[c, 0].astype(F32))

    @pl.loop(PAIR_FIRST, CHUNKS)
    def _(c):
        ring_pair(c).wait_recv()
        finish(c, q[c, z, y].astype(F32) + yr[c].astype(F32))

    g3.wait_recv()
    win_ref[...] = (gx[x, yh].astype(F32) + gyr[...].astype(F32)).astype(BF16)

    @pl.loop(0, PAIR_FIRST)
    def _(c):
        pair_copy(c).wait_send()
        for copy in pair_ring1(c) + pair_ring2(c):
            copy.wait_send()

    @pl.loop(PAIR_FIRST, CHUNKS)
    def _(c):
        ring_pair(c).wait_send()
        for copy in ring1(c) + ring2(c):
            copy.wait_send()

    for copy in (core_copy, g1a, g1b, g2a, g2b, g3):
        copy.wait_send()

    @pl.loop(1, 8)
    def _(k):
        emb_copy(k).wait_send()

    gather_sent(texts, text_ss, text_rs)
    gather_sent(msgs, msg_ss, msg_rs)


def body(tokens, w_in, w_out, text_emb, labels, logit_scale, logit_bias):
    vmem = pl.BlockSpec(memory_space=pltpu.VMEM)
    smem = pl.BlockSpec(memory_space=pltpu.SMEM)
    hbm = pl.BlockSpec(memory_space=pl.ANY)
    msg = D + HID + 256
    scratch = [
        pltpu.VMEM((ROWS, D), BF16),
        pltpu.VMEM((ROWS, 1), F32),
        pltpu.VMEM((ROWS, HID), F32),
        pltpu.VMEM((ROWS, HID), BF16),
        pltpu.VMEM((D, ROWS), BF16),
        pltpu.VMEM((D, HID), BF16),
        pltpu.VMEM((HID, D), BF16),
        pltpu.VMEM((IMGS, D), F32),
        pltpu.VMEM((IMGS, HID), F32),
        pltpu.VMEM((IMGS, HID), F32),
        pltpu.VMEM((16, HALF), F32),
        pltpu.VMEM((1, HID), F32),
        pltpu.VMEM((TOKS, 128), F32),
        pltpu.VMEM((TOKS, 128), F32),
        pltpu.VMEM((256, HALF), F32),
        pltpu.VMEM((16, 16, HALF), BF16),
        pltpu.VMEM((8, 16, HALF), BF16),
        pltpu.VMEM((16, 16, msg), BF16),
        pltpu.VMEM((CHUNKS, 4, 2, 192, TOKS), BF16),
        pltpu.VMEM((CHUNKS, 192, TOKS), BF16),
        pltpu.VMEM((CHUNKS, 192, TOKS), BF16),
        pltpu.VMEM((CHUNKS, 2, 192, TOKS), BF16),
        pltpu.VMEM((CHUNKS, 2, 192, TOKS), BF16),
        pltpu.VMEM((CHUNKS, 192, TOKS), BF16),
        pltpu.VMEM((max(PAIR_FIRST, 1), 4, 192, TOKS), BF16),
        pltpu.VMEM((4, 2, 2, 96, HID), BF16),
        pltpu.VMEM((4, 2, 96, HID), BF16),
        pltpu.VMEM((4, 2, 96, HID), BF16),
        pltpu.VMEM((96, HID), BF16),
        pltpu.VMEM((96, HID), BF16),
        pltpu.VMEM((2, 96, HID), BF16),
        pltpu.VMEM((2, 96, HID), BF16),
        pltpu.VMEM((96, HID), BF16),
        pltpu.SemaphoreType.DMA((CHUNKS,)),
        pltpu.SemaphoreType.DMA((2,)),
        pltpu.SemaphoreType.DMA((2, 8)),
        pltpu.SemaphoreType.DMA((16,)),
        pltpu.SemaphoreType.DMA((8,)),
        pltpu.SemaphoreType.DMA((8,)),
        pltpu.SemaphoreType.DMA((2, 8)),
        pltpu.SemaphoreType.DMA((16,)),
        pltpu.SemaphoreType.DMA((CHUNKS, 7)),
        pltpu.SemaphoreType.DMA((CHUNKS, 7)),
        pltpu.SemaphoreType.DMA((6,)),
        pltpu.SemaphoreType.DMA((6,)),
    ]
    return pl.pallas_call(
        kernel,
        out_shape=(
            jax.ShapeDtypeStruct((ROWS, D // 8), BF16),
            jax.ShapeDtypeStruct((D // 16, HID), BF16),
            jax.ShapeDtypeStruct((HID, D // 16), BF16),
            jax.ShapeDtypeStruct((IMGS, D), BF16),
        ),
        in_specs=[hbm, hbm, hbm, vmem, smem, smem, smem],
        out_specs=(vmem, vmem, vmem, vmem),
        scratch_shapes=scratch,
        compiler_params=pltpu.CompilerParams(
            collective_id=0, has_side_effects=True, vmem_limit_bytes=61 * 2**20
        ),
        cost_estimate=pl.CostEstimate(
            flops=6 * ROWS * D * HID, bytes_accessed=14 * 2**20, transcendentals=2 * ROWS * HID
        ),
    )(tokens, w_in, w_out, text_emb, labels, logit_scale, logit_bias)


def solution(mesh):
    in_specs = (
        P("dp", None),
        P(None, "tensor"),
        P("tensor", None),
        P("dp", None),
        P("dp"),
        P(),
        P(),
    )
    out_specs = (P("dp", "tensor"), P("dp", "tensor"), P("tensor", "dp"), P("dp", None))
    return jax.shard_map(body, mesh=mesh, in_specs=in_specs, out_specs=out_specs, check_vma=False)
```

time: 610 us -> 109 us (0.18)
  waiting for transfers between devices: 369 us -> 0 us
  Pallas kernels: 0 us -> 98.9 us
  matrix products: 79 us -> 0 us
  blocking collectives: 69 us -> 0 us
  other arithmetic: 47.2 us -> 0 us
  local copies, waits for them, and re-layouts: 28.7 us -> 6.1 us
  between operations: 13.9 us -> 1.94 us
    reduce_scatter x3 -> x0, waiting for transfers between devices: 269 us -> none  [the longest x1 130 us: body(): lax.psum_scatter(partial_feats.astype(jnp.bfloat16), 'tensor', scatter_di...]
    ppermute x32 -> x0, waiting for transfers between devices: 99.8 us -> none  [shifted(): return lax.ppermute(block, axis, route)]
    pallas_call x0 -> x1, Pallas kernels: none -> 98.9 us  [body(): pl.pallas_call(kernel, out_shape=(jax.ShapeDtypeStruct((ROWS, D // 8), BF...]
    dot_general x54 -> x0, matrix products: 79 us -> none  [the longest x16 22.8 us: sig_grads(): jnp.dot(image_bf, text_bf.T, preferred_element_type=jnp.float32)]
    psum x2 -> x0, blocking collectives: 69 us -> none  [the longest x1 36.4 us: body(): lax.psum(jnp.dot(pooled_bf, w_out, preferred_element_type=jnp.float32), '...]
    unnamed x21 -> x4, local copies, waits for them, and re-layouts: 28.1 us -> 2.19 us
    convert_element_type x7 -> x0, other arithmetic: 19.9 us -> none  [the longest x1 6.33 us: body(): jax.vjp(jax.nn.gelu, hidden_pre)[1](spread)[0].astype(jnp.bfloat16)]
    reduce_sum x8 -> x0, other arithmetic: 17.5 us -> none  [the longest x1 6.28 us: body(): jnp.mean(tokens.astype(jnp.float32).reshape(local_images, TOKS, width), a...]
  transfers between devices with their start and end apart: 35 -> 0, of which waited for: 35 -> 0; matrix products, arithmetic and copies ran while one was open for 13% -> 0% of each run, Pallas kernels for 0% -> 0%
where the time goes in v1:
time: 109 us; the launch traced here: 107 us
  Pallas kernels  98.9 us (91%)
  local copies, waits for them, and re-layouts  6.1 us (6%)
  between operations  1.94 us (2%)
    pallas_call x1, Pallas kernels, body(): pl.pallas_call(kernel, out_shape=(jax.ShapeDtypeStruct((ROWS, D // 8), BF...  98.9 us
    pallas_call x2, local copies, waits for them, and re-layouts, body(): pl.pallas_call(kernel, out_shape=(jax.ShapeDtypeStruct((ROWS, D // 8), BF...  3.91 us
    unnamed x4, local copies, waits for them, and re-layouts  2.19 us

profile of v1, /device:TPU:0, one launch (start us, length us, event | category | flops | bytes accessed | tf_op | source)
XLA Modules:
  0.0 107.0 jit_solution(6713919964661667247)
XLA Ops:
  1.9 98.9 %shard_map.102 = (bf16[2048,192]{1,0:T(8,128)(2,1)}, bf16[96,768]{1,0:T(8,128)(2,1)}, bf16[768,96]{1,0:T(8,128)(2,1)}, bf16[8,1536]{1,0:T(8,128)(2,1)}) custom-call(bf16[2048,1536]{1,0:T(8,128)(2,1)} %tokens_hbm.1, bf16[1536,768]{1,0:T(8,128)(2,1)} %w_in_hbm.1, bf16[768,1536]{1,0:T(8,128)(2,1)} %w_out_hbm.1, bf16[8,1536]{1,0:T(8,128)(2,1)} %text_ref.1, ...), custom_call_target="tpu_custom_call" | custom-call | flops 14495514624 | bytes 14680064 | tf_op jit(solution)/shard_map/pallas_call | solution.py:550
  100.9 0.0 copy-start
  100.9 2.2 %copy.11 = bf16[2048,192]{0,1:T(8,128)(2,1)} copy(bf16[2048,192]{1,0:T(8,128)(2,1)} %get-tuple-element.4) | data formatting | bytes 1572864 | tf_op jit(solution)/shard_map/pallas_call | solution.py:550
  103.1 1.7 %copy.12 = bf16[768,96]{0,1:T(8,128)(2,1)} copy(bf16[768,96]{1,0:T(8,128)(2,1)} %get-tuple-element.6) | data formatting | bytes 294912 | tf_op jit(solution)/shard_map/pallas_call | solution.py:550
  104.8 1.6 %copy.17 = bf16[96,768]{1,0:T(8,128)(2,1)} copy(bf16[96,768]{1,0:T(8,128)(2,1)} %get-tuple-element.13) | data formatting | bytes 294912
  106.4 0.0 copy-done
  106.4 0.6 copy.18
Async XLA Ops:
  100.9 5.5 %copy-start = (bf16[8,1536]{1,0:T(8,128)(2,1)S(1)}, bf16[8,1536]{1,0:T(8,128)(2,1)}, u32[]{:S(2)}) copy-start(bf16[8,1536]{1,0:T(8,128)(2,1)} %get-tuple-element.15) | copy-start | bytes 73732

commit v2 on v1

v2 whole, which is shorter than its diff:
```python
import math

import jax
import jax.numpy as jnp
from jax import lax
from jax.experimental import pallas as pl
from jax.experimental.pallas import tpu as pltpu
from jax.sharding import PartitionSpec as P

F32 = jnp.float32
BF16 = jnp.bfloat16

D = 1536
HALF = D // 2
HID = 768
ROWS = 2048
TOKS = 256
IMGS = 8
LOSS_SCALE = 64.0
EPS = 1e-06
GELU_A = math.sqrt(2.0 / math.pi)
GELU_B = 0.044715

CHUNKS = 8
GROUPS = ((0, 4), (4, 8))
PAIR_FIRST = (1, 3, 5)

NN = (((1,), (0,)), ((), ()))
NT = (((1,), (1,)), ((), ()))
TN = (((0,), (0,)), ((), ()))


def dot(a, b, dims=NN):
    return lax.dot_general(a, b, dims, preferred_element_type=F32)


def kernel(
    tokens_hbm, w_in_hbm, w_out_hbm, text_ref, labels_ref, scale_ref, bias_ref,
    out_hbm, win_hbm, wout_hbm, tgrad_hbm,
    tok, inv, minv, hpre, hg, nt, w_in, w_out,
    tmean, pooled, pgs, egs, csum, inv_t, eg_t, tdir,
    texts, ebuf, msgs,
    q, ra, rb, sa, sb, yr, yq,
    g, gc, gx, gra, grb, gsa, gsb, gyr,
    out, win, wout, tgrad,
    tok_sem, w_sem,
    text_ss, text_rs, emb_ss, emb_rs, msg_ss, msg_rs,
    q_ss, q_rs, g_ss, g_rs, out_sem,
):
    dp = lax.axis_index("dp")
    tp = lax.axis_index("tensor")
    yh, local = dp // 8, dp % 8
    x, core = local // 2, dp % 2
    z, y = tp // 2, tp % 2

    def mesh_z(step):
        return (dp, ((z + step) % 4) * 2 + y)

    def mesh_x(step):
        return (yh * 8 + ((x + step) % 4) * 2 + core, tp)

    y_pair = (dp, z * 2 + (1 - y))
    core_pair = (dp - core + (1 - core), tp)
    y_far = ((1 - yh) * 8 + local, tp)

    def octet(k):
        return (yh * 8 + (local + k) % 8, tp)

    def remote(src, dst, ssem, rsem, dev):
        return pltpu.make_async_remote_copy(
            src_ref=src, dst_ref=dst, send_sem=ssem, recv_sem=rsem,
            device_id=dev, device_id_type=pl.DeviceIdType.MESH,
        )

    def tok_copy(c):
        rows = pl.ds(c * TOKS, TOKS)
        return pltpu.make_async_copy(tokens_hbm.at[rows], tok.at[rows], tok_sem.at[c])

    tok_copy(0).start()
    w_in_copy = pltpu.make_async_copy(w_in_hbm, w_in, w_sem.at[0])
    w_out_copy = pltpu.make_async_copy(w_out_hbm, w_out, w_sem.at[1])
    w_in_copy.start()
    for c in range(1, CHUNKS):
        tok_copy(c).start()
    w_out_copy.start()

    barrier = pltpu.get_barrier_semaphore()

    def greet(dev):
        pl.semaphore_signal(barrier, inc=1, device_id=dev, device_id_type=pl.DeviceIdType.MESH)

    greet(y_far)
    for k in range(1, 8):
        greet(octet(k))
        greet((dp, (tp + k) % 8))

    text_vals = text_ref[...].astype(F32)
    text_inv = lax.rsqrt(jnp.sum(text_vals * text_vals, axis=1, keepdims=True) + EPS)
    text_nrm = text_vals * text_inv
    texts[dp] = jnp.concatenate([text_nrm[:, :HALF], text_nrm[:, HALF:]], axis=0).astype(BF16)
    tmean[...] = jnp.zeros_like(tmean)
    pooled[...] = jnp.zeros_like(pooled)

    def gather_send(buf, slot, ss, rs, row):
        @pl.loop(1, 8)
        def _(k):
            remote(buf.at[slot], buf.at[slot], ss.at[row, k], rs.at[slot], octet(k)).start()

    def gather_far(buf, ss, rs):
        return remote(buf.at[dp], buf.at[dp], ss.at[0, 0], rs.at[dp], y_far)

    def gather_recv(buf, slot, ss, rs):
        remote(buf.at[slot], buf.at[slot], ss.at[0, 0], rs.at[slot], y_far).wait_recv()

    def gather_first(buf, ss, rs):
        gather_far(buf, ss, rs).start()
        gather_send(buf, dp, ss, rs, 0)

    far_slot = (1 - yh) * 8 + local

    def gather_relay(buf, ss, rs):
        gather_recv(buf, far_slot, ss, rs)
        gather_send(buf, far_slot, ss, rs, 1)

    def gather_rest(buf, ss, rs):
        @pl.loop(1, 8)
        def _(k):
            gather_recv(buf, yh * 8 + (local + k) % 8, ss, rs)
            gather_recv(buf, (1 - yh) * 8 + (local + k) % 8, ss, rs)

    def gather_sent(buf, ss, rs):
        gather_far(buf, ss, rs).wait_send()

        @pl.loop(1, 8)
        def _(k):
            for row in range(2):
                remote(buf.at[dp], buf.at[dp], ss.at[row, k], rs.at[dp], octet(k)).wait_send()

    def project(c):
        rows = pl.ds(c * TOKS, TOKS)
        hpre[rows, :] = dot(tok[rows, :], w_in[...])

    def statistics(c):
        acc = jnp.zeros((8, D), F32)
        for b in range(TOKS // 16):
            rows = pl.ds(c * TOKS + b * 16, 16)
            vals = tok[rows, :].astype(F32)
            mean = jnp.sum(vals, axis=1, keepdims=True) * (1.0 / D)
            center = vals - mean
            var = jnp.sum(center * center, axis=1, keepdims=True) * (1.0 / D)
            scale = lax.rsqrt(var + EPS)
            inv[rows, :] = scale
            minv[rows, :] = mean * scale
            acc = acc + (vals[:8] + vals[8:])
        tmean[pl.ds(c, 1), :] = jnp.sum(acc, axis=0, keepdims=True) * (1.0 / TOKS)

    def pool(c):
        cs = csum[...]
        acc = jnp.zeros((8, HID), F32)
        for b in range(TOKS // 16):
            rows = pl.ds(c * TOKS + b * 16, 16)
            h = hpre[rows, :] * inv[rows, :] - minv[rows, :] * cs
            hpre[rows, :] = h
            t = jnp.tanh(h * (GELU_A + (GELU_A * GELU_B) * (h * h)))
            act = h + h * t
            acc = acc + (act[:8] + act[8:])
        pooled[pl.ds(c, 1), :] = jnp.sum(acc, axis=0, keepdims=True) * (0.5 / TOKS)

    def forward(first, last):
        for c in range(first, last):
            project(c)
            statistics(c)
            if c > first:
                pool(c - 1)
        pool(last - 1)

    def emb_copy(n, k):
        return remote(
            ebuf.at[n, tp], ebuf.at[n, tp], emb_ss.at[n, k], emb_rs.at[n, tp], (dp, (tp + k) % 8)
        )

    def exchange_start(n):
        part = dot(pooled[...].astype(BF16), w_out[...])
        ebuf[n, tp] = jnp.concatenate([part[:, :HALF], part[:, HALF:]], axis=0).astype(BF16)

        @pl.loop(1, 8)
        def _(k):
            emb_copy(n, k).start()

    def exchange_wait(n):
        @pl.loop(1, 8)
        def _(k):
            src = (tp + k) % 8
            remote(
                ebuf.at[n, src], ebuf.at[n, src], emb_ss.at[n, k], emb_rs.at[n, src], (dp, src)
            ).wait_recv()

    def flip(c):
        rows = pl.ds(c * TOKS, TOKS)
        scale = inv[rows, :]
        normed = (tok[rows, :].astype(F32) * scale - minv[rows, :]).astype(BF16)
        nt[:, rows] = normed.T
        inv_t[pl.ds(c, 1), :] = jnp.broadcast_to(scale, (TOKS, 128)).T[0:1, :]

    def both(sums):
        total = sums[:IMGS] + sums[IMGS:]
        return jnp.concatenate([total, total], axis=0)

    scale = scale_ref[0]

    def loss(n):
        tm = tmean[...]
        emb = jnp.concatenate([tm[:, :HALF], tm[:, HALF:]], axis=0)
        for k in range(8):
            emb = emb + ebuf[n, k].astype(F32)
        emb_inv = lax.rsqrt(both(jnp.sum(emb * emb, axis=1, keepdims=True)) + EPS)
        image_bf = (emb * emb_inv).astype(BF16)
        text_all = texts[...].reshape(256, HALF)
        prod = dot(image_bf, text_all, NT)
        logits = scale * (prod[:IMGS] + pltpu.roll(prod[IMGS:], 256 - IMGS, 1)) + bias_ref[0]
        lane = lax.broadcasted_iota(jnp.int32, (IMGS, 256), 1)
        row = lax.broadcasted_iota(jnp.int32, (IMGS, 256), 0)
        valid = (lane % 16) < 8
        text_id = (lane // 16) * 8 + lane % 16
        label = jnp.zeros((IMGS, 256), jnp.int32)
        for k in range(IMGS):
            label = jnp.where(row == k, labels_ref[k], label)
        signs = jnp.where(label == text_id, 1.0, -1.0)
        grad = -signs * jax.nn.sigmoid(-signs * logits) * LOSS_SCALE
        grad = jnp.where(valid, grad, 0.0)
        grad = jnp.concatenate([grad, pltpu.roll(grad, IMGS, 1)], axis=0).astype(BF16)
        image_dir = scale * dot(grad, text_all)
        emb_grad = emb_inv * image_dir - (emb_inv * emb_inv * emb_inv) * emb * both(
            jnp.sum(emb * image_dir, axis=1, keepdims=True)
        )
        eg_bf = emb_grad.astype(BF16)
        pgs[...] = (
            dot(eg_bf[:IMGS], w_out[:, :HALF], NT) + dot(eg_bf[IMGS:], w_out[:, HALF:], NT)
        ) * (1.0 / TOKS)
        if n == len(GROUPS) - 1:
            egs[...] = emb_grad * (1.0 / TOKS)
            msgs[dp, :, 0:HALF] = image_bf
            msgs[dp, :, HALF:D] = eg_bf
            pooled_f = pooled[...]
            msgs[dp, :, D:D + HID] = jnp.concatenate([pooled_f, pooled_f], axis=0).astype(BF16)
            msgs[dp, :, D + HID:D + HID + 256] = grad

    def hidden_chunk(c):
        pg = pgs[pl.ds(c, 1), :]
        cs = csum[...]
        first, second = [], []
        for b in range(TOKS // 16):
            rows = pl.ds(c * TOKS + b * 16, 16)
            h = hpre[rows, :]
            h2 = h * h
            t = jnp.tanh(h * (GELU_A + (GELU_A * GELU_B) * h2))
            slope = (1.0 + t) + h * (1.0 - t * t) * (GELU_A + (3.0 * GELU_A * GELU_B) * h2)
            grad_bf = (slope * (0.5 * pg)).astype(BF16)
            hg[rows, :] = grad_bf
            grad_h = grad_bf.astype(F32)
            p1 = grad_h * cs
            p2 = grad_h * h
            s1 = p1[:, 0:128]
            s2 = p2[:, 0:128]
            for i in range(1, HID // 128):
                s1 = s1 + p1[:, i * 128:(i + 1) * 128]
                s2 = s2 + p2[:, i * 128:(i + 1) * 128]
            first.append(s1)
            second.append(s2)
        m1 = jnp.sum(jnp.concatenate(first, axis=0).T, axis=0, keepdims=True) * (1.0 / D)
        m2 = jnp.sum(jnp.concatenate(second, axis=0).T, axis=0, keepdims=True) * (1.0 / D)
        rows = pl.ds(c * TOKS, TOKS)
        hgc = hg[rows, :]
        for zb in range(4):
            feats = pl.ds(zb * 384, 384)
            block = dot(w_in[feats, :], hgc, NT) - m1 - nt[feats, rows].astype(F32) * m2
            block = block.astype(BF16)
            q[c, zb, 0] = block[:192]
            q[c, zb, 1] = block[192:]

    zp, zn, zo = (z + 1) % 4, (z + 3) % 4, (z + 2) % 4
    up, down = mesh_z(1), mesh_z(3)
    lo, hi = pl.ds(0, 96), pl.ds(96, 96)

    def add_into(dst, a, b):
        dst[...] = (a[...].astype(F32) + b[...].astype(F32)).astype(BF16)

    def pair_copy(c):
        n = PAIR_FIRST.index(c)
        return remote(q.at[c, :, 1 - y], yq.at[n], q_ss.at[c, 0], q_rs.at[c, 0], y_pair)

    def pair_ring1(c):
        return (
            remote(q.at[c, zo, y, lo], ra.at[c, lo], q_ss.at[c, 1], q_rs.at[c, 1], up),
            remote(q.at[c, zo, y, hi], rb.at[c, lo], q_ss.at[c, 2], q_rs.at[c, 2], down),
            remote(q.at[c, zp, y, hi], sa.at[c, 0, hi], q_ss.at[c, 3], q_rs.at[c, 3], up),
            remote(q.at[c, zn, y, lo], sb.at[c, 0, lo], q_ss.at[c, 4], q_rs.at[c, 4], down),
        )

    def pair_ring2(c):
        return (
            remote(q.at[c, zp, y, lo], sa.at[c, 0, lo], q_ss.at[c, 5], q_rs.at[c, 5], up),
            remote(q.at[c, zn, y, hi], sb.at[c, 0, hi], q_ss.at[c, 6], q_rs.at[c, 6], down),
        )

    def ring1(c):
        return (
            remote(q.at[c, zo, 0], ra.at[c], q_ss.at[c, 1], q_rs.at[c, 1], up),
            remote(q.at[c, zo, 1], rb.at[c], q_ss.at[c, 2], q_rs.at[c, 2], down),
            remote(q.at[c, zp, 1], sa.at[c, 1], q_ss.at[c, 3], q_rs.at[c, 3], up),
            remote(q.at[c, zn, 0], sb.at[c, 0], q_ss.at[c, 4], q_rs.at[c, 4], down),
        )

    def ring2(c):
        return (
            remote(q.at[c, zp, 0], sa.at[c, 0], q_ss.at[c, 5], q_rs.at[c, 5], up),
            remote(q.at[c, zn, 1], sb.at[c, 1], q_ss.at[c, 6], q_rs.at[c, 6], down),
        )

    def ring_pair(c):
        return remote(q.at[c, z, 1 - y], yr.at[c], q_ss.at[c, 0], q_rs.at[c, 0], y_pair)

    def start(copies):
        for copy in copies:
            copy.start()

    def step_a(c):
        hidden_chunk(c)
        start((pair_copy(c),) if c in PAIR_FIRST else ring1(c))

    def step_b(c):
        if c in PAIR_FIRST:
            pair_copy(c).wait_recv()
            for zb in range(4):
                blk = q.at[c, zb, y]
                add_into(blk, blk, yq.at[PAIR_FIRST.index(c), zb])
            start(pair_ring1(c))
        else:
            first, second = ring1(c)[:2]
            first.wait_recv()
            add_into(q.at[c, zp, 0], q.at[c, zp, 0], ra.at[c])
            second.wait_recv()
            add_into(q.at[c, zn, 1], q.at[c, zn, 1], rb.at[c])
            start(ring2(c))

    def step_c(c):
        if c in PAIR_FIRST:
            first, second = pair_ring1(c)[:2]
            first.wait_recv()
            add_into(q.at[c, zp, y, lo], q.at[c, zp, y, lo], ra.at[c, lo])
            second.wait_recv()
            add_into(q.at[c, zn, y, hi], q.at[c, zn, y, hi], rb.at[c, lo])
            start(pair_ring2(c))
        else:
            for copy in ring1(c)[2:] + ring2(c):
                copy.wait_recv()
            for half in range(2):
                blk = q.at[c, z, half]
                blk[...] = (
                    blk[...].astype(F32) + sa[c, half].astype(F32) + sb[c, half].astype(F32)
                ).astype(BF16)
            ring_pair(c).start()

    def out_copy(c):
        rows = pl.ds(c * TOKS, TOKS)
        return pltpu.make_async_copy(out.at[:, rows], out_hbm.at[:, rows], out_sem.at[c])

    def step_d(c):
        if c in PAIR_FIRST:
            for copy in pair_ring1(c)[2:] + pair_ring2(c):
                copy.wait_recv()
            total = q[c, z, y].astype(F32) + sa[c, 0].astype(F32) + sb[c, 0].astype(F32)
        else:
            ring_pair(c).wait_recv()
            total = q[c, z, y].astype(F32) + yr[c].astype(F32)
        rows = pl.ds(c * TOKS, TOKS)
        out[:, rows] = (
            inv_t[pl.ds(c, 1), :] * total + eg_t[0:192, c:c + 1]
        ).astype(BF16)
        out_copy(c).start()

    xp, xn, xo = (x + 1) % 4, (x + 3) % 4, (x + 2) % 4
    right, left = mesh_x(1), mesh_x(3)

    core_copy = remote(g.at[:, :, 1 - core], gc, g_ss.at[0], g_rs.at[0], core_pair)
    g1a = remote(gx.at[xo, 0], gra, g_ss.at[1], g_rs.at[1], right)
    g1b = remote(gx.at[xo, 1], grb, g_ss.at[2], g_rs.at[2], left)
    g2a = remote(gx.at[xp], gsa, g_ss.at[3], g_rs.at[3], right)
    g2b = remote(gx.at[xn], gsb, g_ss.at[4], g_rs.at[4], left)
    g3 = remote(gx.at[x, 1 - yh], gyr, g_ss.at[5], g_rs.at[5], y_far)

    def weight_a():
        @pl.loop(0, 4)
        def _(i):
            feats = pl.ds(pl.multiple_of(i * 384, 384), 384)
            block = dot(nt[feats, :], hg[...]).astype(BF16)
            for k in range(4):
                g[i, k // 2, k % 2] = block[k * 96:(k + 1) * 96]

        core_copy.start()

    def weight_b():
        core_copy.wait_recv()

        @pl.loop(0, 8)
        def _(k):
            xb, yb = k // 2, k % 2
            i, j = yb * 2 + xb // 2, xb % 2
            add_into(gx.at[xb, yb], g.at[i, j, core], gc.at[i, j])

        g1a.start()
        g1b.start()

    def weight_c():
        g1a.wait_recv()
        add_into(gx.at[xp, 0], gx.at[xp, 0], gra)
        g1b.wait_recv()
        add_into(gx.at[xn, 1], gx.at[xn, 1], grb)
        g2a.start()
        g2b.start()

    def weight_d():
        g2a.wait_recv()
        g2b.wait_recv()
        for half in range(2):
            blk = gx.at[x, half]
            blk[...] = (
                blk[...].astype(F32) + gsa[half].astype(F32) + gsb[half].astype(F32)
            ).astype(BF16)
        g3.start()

    def small_out(src, dst, k):
        return pltpu.make_async_copy(src, dst, out_sem.at[CHUNKS + k])

    def weight_e():
        g3.wait_recv()
        win[...] = (gx[x, yh].astype(F32) + gyr[...].astype(F32)).astype(BF16)
        small_out(win, win_hbm, 0).start()

    def gathered():
        gather_rest(msgs, msg_ss, msg_rs)
        all_msgs = msgs[...].reshape(256, D + HID + 256)
        tdir[...] = dot(all_msgs[:, D + HID:], all_msgs[:, :HALF], TN)
        text_dir = scale * tdir[pl.ds(pl.multiple_of(dp * 16, 16), 16), :]
        text_dir = jnp.concatenate([text_dir[:IMGS], text_dir[IMGS:]], axis=1)
        vals = text_ref[...].astype(F32)
        t_inv = lax.rsqrt(jnp.sum(vals * vals, axis=1, keepdims=True) + EPS)
        tgrad[...] = (
            t_inv * text_dir
            - (t_inv * t_inv * t_inv) * vals * jnp.sum(vals * text_dir, axis=1, keepdims=True)
        ).astype(BF16)
        small_out(tgrad, tgrad_hbm, 1).start()
        feat = lax.broadcasted_iota(jnp.int32, (HALF, 128), 0)
        col = lax.broadcasted_iota(jnp.int32, (HALF, 128), 1)
        pick = jnp.where(feat == col + local * 96, 1.0, 0.0).astype(BF16)
        emb_cols = dot(all_msgs[:, HALF:D], pick)
        slot_row = lax.broadcasted_iota(jnp.int32, (256, 128), 0)
        emb_cols = jnp.where((slot_row // 8) % 2 == yh, emb_cols, 0.0).astype(BF16)
        wout[...] = dot(emb_cols, all_msgs[:, D:D + HID], TN)[:96].astype(BF16)
        small_out(wout, wout_hbm, 2).start()

    def own_columns():
        cols = egs[pl.ds(pl.multiple_of((z // 2) * 8, 8), 8),
                   pl.ds(pl.multiple_of((z % 2) * 384, 128), 384)]
        cols = jnp.where(y == 0, cols[:, :192], cols[:, 192:])
        square = jnp.concatenate([cols, jnp.zeros((8, 64), F32)], axis=1)
        square = jnp.concatenate([square, jnp.zeros((120, 256), F32)], axis=0)
        eg_t[...] = square.T

    w_in_copy.wait()
    for c in range(0, 4):
        tok_copy(c).wait()
    csum[...] = dot(jnp.full((16, D), 1.0, BF16), w_in[...])[0:1]
    pl.semaphore_wait(barrier, 15)
    gather_first(texts, text_ss, text_rs)
    forward(*GROUPS[0])
    w_out_copy.wait()
    exchange_start(0)
    gather_relay(texts, text_ss, text_rs)
    for c in range(*GROUPS[0]):
        flip(c)
    exchange_wait(0)
    gather_rest(texts, text_ss, text_rs)
    loss(0)
    for c in range(*GROUPS[0]):
        step_a(c)

    for c in range(4, CHUNKS):
        tok_copy(c).wait()
    forward(*GROUPS[1])
    exchange_start(1)
    step_b(0)
    for c in range(*GROUPS[1]):
        flip(c)
    step_b(1)
    exchange_wait(1)
    loss(1)
    step_b(2)
    step_a(4)
    gather_first(msgs, msg_ss, msg_rs)
    step_c(0)
    step_a(5)
    step_b(3)
    step_a(6)
    step_c(2)
    step_a(7)
    step_c(1)
    own_columns()
    weight_a()
    gather_relay(msgs, msg_ss, msg_rs)
    step_b(4)
    step_c(3)
    weight_b()
    step_d(0)
    step_b(6)
    step_b(7)
    step_b(5)
    step_d(2)
    weight_c()
    gathered()
    step_c(4)
    step_d(1)
    step_d(3)
    weight_d()
    step_c(6)
    step_c(7)
    step_c(5)
    step_d(4)
    weight_e()
    step_d(6)
    step_d(7)
    step_d(5)

    for c in range(CHUNKS):
        if c in PAIR_FIRST:
            copies = (pair_copy(c),) + pair_ring1(c) + pair_ring2(c)
        else:
            copies = (ring_pair(c),) + ring1(c) + ring2(c)
        for copy in copies:
            copy.wait_send()
    for copy in (core_copy, g1a, g1b, g2a, g2b, g3):
        copy.wait_send()
    for n in range(len(GROUPS)):
        @pl.loop(1, 8)
        def _(k):
            emb_copy(n, k).wait_send()

    gather_sent(texts, text_ss, text_rs)
    gather_sent(msgs, msg_ss, msg_rs)
    for c in range(CHUNKS):
        out_copy(c).wait()
    small_out(win, win_hbm, 0).wait()
    small_out(tgrad, tgrad_hbm, 1).wait()
    small_out(wout, wout_hbm, 2).wait()


def hand_out(a, b, c, d, a_out, b_out, c_out, d_out, sem):
    copies = [
        pltpu.make_async_copy(src, dst, sem.at[k])
        for k, (src, dst) in enumerate(((a, a_out), (b, b_out), (c, c_out), (d, d_out)))
    ]
    for copy in copies:
        copy.start()
    for copy in copies:
        copy.wait()


def body(tokens, w_in, w_out, text_emb, labels, logit_scale, logit_bias):
    vmem = pl.BlockSpec(memory_space=pltpu.VMEM)
    smem = pl.BlockSpec(memory_space=pltpu.SMEM)
    hbm = pl.BlockSpec(memory_space=pl.ANY)
    msg = D + HID + 256
    groups = len(GROUPS)
    scratch = [
        pltpu.VMEM((ROWS, D), BF16),
        pltpu.VMEM((ROWS, 1), F32),
        pltpu.VMEM((ROWS, 1), F32),
        pltpu.VMEM((ROWS, HID), F32),
        pltpu.VMEM((ROWS, HID), BF16),
        pltpu.VMEM((D, ROWS), BF16),
        pltpu.VMEM((D, HID), BF16),
        pltpu.VMEM((HID, D), BF16),
        pltpu.VMEM((IMGS, D), F32),
        pltpu.VMEM((IMGS, HID), F32),
        pltpu.VMEM((IMGS, HID), F32),
        pltpu.VMEM((16, HALF), F32),
        pltpu.VMEM((1, HID), F32),
        pltpu.VMEM((CHUNKS, TOKS), F32),
        pltpu.VMEM((256, 128), F32),
        pltpu.VMEM((256, HALF), F32),
        pltpu.VMEM((16, 16, HALF), BF16),
        pltpu.VMEM((groups, 8, 16, HALF), BF16),
        pltpu.VMEM((16, 16, msg), BF16),
        pltpu.VMEM((CHUNKS, 4, 2, 192, TOKS), BF16),
        pltpu.VMEM((CHUNKS, 192, TOKS), BF16),
        pltpu.VMEM((CHUNKS, 192, TOKS), BF16),
        pltpu.VMEM((CHUNKS, 2, 192, TOKS), BF16),
        pltpu.VMEM((CHUNKS, 2, 192, TOKS), BF16),
        pltpu.VMEM((CHUNKS, 192, TOKS), BF16),
        pltpu.VMEM((len(PAIR_FIRST), 4, 192, TOKS), BF16),
        pltpu.VMEM((4, 2, 2, 96, HID), BF16),
        pltpu.VMEM((4, 2, 96, HID), BF16),
        pltpu.VMEM((4, 2, 96, HID), BF16),
        pltpu.VMEM((96, HID), BF16),
        pltpu.VMEM((96, HID), BF16),
        pltpu.VMEM((2, 96, HID), BF16),
        pltpu.VMEM((2, 96, HID), BF16),
        pltpu.VMEM((96, HID), BF16),
        pltpu.VMEM((192, ROWS), BF16),
        pltpu.VMEM((96, HID), BF16),
        pltpu.VMEM((96, HID), BF16),
        pltpu.VMEM((IMGS, D), BF16),
        pltpu.SemaphoreType.DMA((CHUNKS,)),
        pltpu.SemaphoreType.DMA((2,)),
        pltpu.SemaphoreType.DMA((2, 8)),
        pltpu.SemaphoreType.DMA((16,)),
        pltpu.SemaphoreType.DMA((groups, 8)),
        pltpu.SemaphoreType.DMA((groups, 8)),
        pltpu.SemaphoreType.DMA((2, 8)),
        pltpu.SemaphoreType.DMA((16,)),
        pltpu.SemaphoreType.DMA((CHUNKS, 7)),
        pltpu.SemaphoreType.DMA((CHUNKS, 7)),
        pltpu.SemaphoreType.DMA((6,)),
        pltpu.SemaphoreType.DMA((6,)),
        pltpu.SemaphoreType.DMA((CHUNKS + 3,)),
    ]
    shapes = (
        jax.ShapeDtypeStruct((D // 8, ROWS), BF16),
        jax.ShapeDtypeStruct((D // 16, HID), BF16),
        jax.ShapeDtypeStruct((D // 16, HID), BF16),
        jax.ShapeDtypeStruct((IMGS, D), BF16),
    )
    results = pl.pallas_call(
        kernel,
        out_shape=shapes,
        in_specs=[hbm, hbm, hbm, vmem, smem, smem, smem],
        out_specs=(hbm, hbm, hbm, hbm),
        scratch_shapes=scratch,
        compiler_params=pltpu.CompilerParams(
            collective_id=0, has_side_effects=True, vmem_limit_bytes=61 * 2**20
        ),
        cost_estimate=pl.CostEstimate(
            flops=6 * ROWS * D * HID, bytes_accessed=14 * 2**20, transcendentals=2 * ROWS * HID
        ),
    )(tokens, w_in, w_out, text_emb, labels, logit_scale, logit_bias)
    token_t, w_in_grad, w_out_t, text_grad = pl.pallas_call(
        hand_out,
        out_shape=shapes,
        in_specs=[hbm, hbm, hbm, hbm],
        out_specs=(hbm, hbm, hbm, hbm),
        scratch_shapes=[pltpu.SemaphoreType.DMA((4,))],
        compiler_params=pltpu.CompilerParams(vmem_limit_bytes=61 * 2**20),
        cost_estimate=pl.CostEstimate(flops=0, bytes_accessed=2 * 2**20, transcendentals=0),
    )(*results)
    return token_t.T, w_in_grad, w_out_t.T, text_grad


def solution(mesh):
    in_specs = (
        P("dp", None),
        P(None, "tensor"),
        P("tensor", None),
        P("dp", None),
        P("dp"),
        P(),
        P(),
    )
    out_specs = (P("dp", "tensor"), P("dp", "tensor"), P("tensor", "dp"), P("dp", None))
    return jax.shard_map(body, mesh=mesh, in_specs=in_specs, out_specs=out_specs, check_vma=False)
```

time: 109 us -> 126 us (1.16)
  Pallas kernels: 98.9 us -> 122 us
  local copies, waits for them, and re-layouts: 6.1 us -> 0 us
    pallas_call x1 -> x2, Pallas kernels: 98.9 us -> 122 us  [the longest x1 87.7 us: body(): pl.pallas_call(kernel, out_shape=shapes, in_specs=[hbm, hbm, hbm, vmem, s...]
    pallas_call x2 -> x0, local copies, waits for them, and re-layouts: 3.91 us -> none  [body(): pl.pallas_call(kernel, out_shape=(jax.ShapeDtypeStruct((ROWS, D // 8), BF...]
    unnamed x4 -> x0, local copies, waits for them, and re-layouts: 2.19 us -> none
where the time goes in v2:
time: 126 us; the launch traced here: 124 us
  Pallas kernels  122 us (97%)
  between operations  2.11 us (2%)
    pallas_call x1, Pallas kernels, body(): pl.pallas_call(kernel, out_shape=shapes, in_specs=[hbm, hbm, hbm, vmem, s...  87.7 us
    pallas_call x1, Pallas kernels, body(): pl.pallas_call(hand_out, out_shape=shapes, in_specs=[hbm, hbm, hbm, hbm],...  34.6 us

profile of v2, /device:TPU:0, one launch (start us, length us, event | category | flops | bytes accessed | tf_op | source)
XLA Modules:
  0.0 124.5 jit_solution(9604777290326947601)
XLA Ops:
  1.9 87.7 %shard_map.102 = (bf16[192,2048]{1,0:T(8,128)(2,1)}, bf16[96,768]{1,0:T(8,128)(2,1)}, bf16[96,768]{1,0:T(8,128)(2,1)}, bf16[8,1536]{1,0:T(8,128)(2,1)}) custom-call(bf16[2048,1536]{1,0:T(8,128)(2,1)} %tokens_hbm.1, bf16[1536,768]{1,0:T(8,128)(2,1)} %w_in_hbm.1, bf16[768,1536]{1,0:T(8,128)(2,1)} %w_out_hbm.1, bf16[8,1536]{1,0:T(8,128)(2,1)} %text_ref.1, ...), custom_call_target="tpu_custom_call" | custom-call | flops 14495514624 | bytes 14680064 | tf_op jit(solution)/shard_map/pallas_call | solution.py:633
  89.7 34.6 %shard_map.103 = (bf16[192,2048]{1,0:T(8,128)(2,1)}, bf16[96,768]{1,0:T(8,128)(2,1)}, bf16[96,768]{1,0:T(8,128)(2,1)}, bf16[8,1536]{1,0:T(8,128)(2,1)}) custom-call(bf16[192,2048]{1,0:T(8,128)(2,1)} %get-tuple-element.12.a, bf16[96,768]{1,0:T(8,128)(2,1)} %get-tuple-element.13.b, bf16[96,768]{1,0:T(8,128)(2,1)} %get-tuple-element.14.c, ...), custom_call_target="tpu_custom_call" | custom-call | bytes 2097152 | tf_op jit(solution)/shard_map/pallas_call | solution.py:646

commit v3 on v2

--- a/solution.py
+++ b/solution.py
@@ -22,8 +22,9 @@
 GELU_B = 0.044715
 
 CHUNKS = 8
-GROUPS = ((0, 4), (4, 8))
-PAIR_FIRST = (1, 3, 5)
+GROUPS = 2
+PER = CHUNKS // GROUPS
+PAIR_FIRST = 3
 
 NN = (((1,), (0,)), ((), ()))
 NT = (((1,), (1,)), ((), ()))
@@ -136,43 +137,40 @@
             for row in range(2):
                 remote(buf.at[dp], buf.at[dp], ss.at[row, k], rs.at[dp], octet(k)).wait_send()
 
-    def project(c):
-        rows = pl.ds(c * TOKS, TOKS)
-        hpre[rows, :] = dot(tok[rows, :], w_in[...])
-
-    def statistics(c):
+    def chunk_rows(c):
+        return pl.ds(pl.multiple_of(c * TOKS, TOKS), TOKS)
+
+    def forward(c):
+        block = tok[chunk_rows(c), :]
+        accs = [dot(block, w_in[:, j * 256:(j + 1) * 256]) for j in range(3)]
+        scales, shifts = [], []
         acc = jnp.zeros((8, D), F32)
         for b in range(TOKS // 16):
-            rows = pl.ds(c * TOKS + b * 16, 16)
+            rows = pl.ds(pl.multiple_of(c * TOKS + b * 16, 16), 16)
             vals = tok[rows, :].astype(F32)
             mean = jnp.sum(vals, axis=1, keepdims=True) * (1.0 / D)
             center = vals - mean
             var = jnp.sum(center * center, axis=1, keepdims=True) * (1.0 / D)
             scale = lax.rsqrt(var + EPS)
+            shift = mean * scale
             inv[rows, :] = scale
-            minv[rows, :] = mean * scale
+            minv[rows, :] = shift
+            scales.append(scale)
+            shifts.append(shift)
             acc = acc + (vals[:8] + vals[8:])
         tmean[pl.ds(c, 1), :] = jnp.sum(acc, axis=0, keepdims=True) * (1.0 / TOKS)
-
-    def pool(c):
-        cs = csum[...]
-        acc = jnp.zeros((8, HID), F32)
-        for b in range(TOKS // 16):
-            rows = pl.ds(c * TOKS + b * 16, 16)
-            h = hpre[rows, :] * inv[rows, :] - minv[rows, :] * cs
-            hpre[rows, :] = h
-            t = jnp.tanh(h * (GELU_A + (GELU_A * GELU_B) * (h * h)))
-            act = h + h * t
-            acc = acc + (act[:8] + act[8:])
-        pooled[pl.ds(c, 1), :] = jnp.sum(acc, axis=0, keepdims=True) * (0.5 / TOKS)
-
-    def forward(first, last):
-        for c in range(first, last):
-            project(c)
-            statistics(c)
-            if c > first:
-                pool(c - 1)
-        pool(last - 1)
+        for j in range(3):
+            cols = slice(j * 256, (j + 1) * 256)
+            cs = csum[:, cols]
+            acc = jnp.zeros((8, 256), F32)
+            for b in range(TOKS // 16):
+                rows = pl.ds(pl.multiple_of(c * TOKS + b * 16, 16), 16)
+                h = accs[j][b * 16:(b + 1) * 16] * scales[b] - shifts[b] * cs
+                hpre[rows, cols] = h
+                t = jnp.tanh(h * (GELU_A + (GELU_A * GELU_B) * (h * h)))
+                act = h + h * t
+                acc = acc + (act[:8] + act[8:])
+            pooled[pl.ds(c, 1), cols] = jnp.sum(acc, axis=0, keepdims=True) * (0.5 / TOKS)
 
     def emb_copy(n, k):
         return remote(
@@ -196,7 +194,7 @@
             ).wait_recv()
 
     def flip(c):
-        rows = pl.ds(c * TOKS, TOKS)
+        rows = chunk_rows(c)
         scale = inv[rows, :]
         normed = (tok[rows, :].astype(F32) * scale - minv[rows, :]).astype(BF16)
         nt[:, rows] = normed.T
@@ -237,20 +235,19 @@
         pgs[...] = (
             dot(eg_bf[:IMGS], w_out[:, :HALF], NT) + dot(eg_bf[IMGS:], w_out[:, HALF:], NT)
         ) * (1.0 / TOKS)
-        if n == len(GROUPS) - 1:
-            egs[...] = emb_grad * (1.0 / TOKS)
-            msgs[dp, :, 0:HALF] = image_bf
-            msgs[dp, :, HALF:D] = eg_bf
-            pooled_f = pooled[...]
-            msgs[dp, :, D:D + HID] = jnp.concatenate([pooled_f, pooled_f], axis=0).astype(BF16)
-            msgs[dp, :, D + HID:D + HID + 256] = grad
+        egs[...] = emb_grad * (1.0 / TOKS)
+        msgs[dp, :, 0:HALF] = image_bf
+        msgs[dp, :, HALF:D] = eg_bf
+        pooled_f = pooled[...]
+        msgs[dp, :, D:D + HID] = jnp.concatenate([pooled_f, pooled_f], axis=0).astype(BF16)
+        msgs[dp, :, D + HID:D + HID + 256] = grad
 
     def hidden_chunk(c):
         pg = pgs[pl.ds(c, 1), :]
         cs = csum[...]
         first, second = [], []
         for b in range(TOKS // 16):
-            rows = pl.ds(c * TOKS + b * 16, 16)
+            rows = pl.ds(pl.multiple_of(c * TOKS + b * 16, 16), 16)
             h = hpre[rows, :]
             h2 = h * h
             t = jnp.tanh(h * (GELU_A + (GELU_A * GELU_B) * h2))
@@ -269,7 +266,7 @@
             second.append(s2)
         m1 = jnp.sum(jnp.concatenate(first, axis=0).T, axis=0, keepdims=True) * (1.0 / D)
         m2 = jnp.sum(jnp.concatenate(second, axis=0).T, axis=0, keepdims=True) * (1.0 / D)
-        rows = pl.ds(c * TOKS, TOKS)
+        rows = chunk_rows(c)
         hgc = hg[rows, :]
         for zb in range(4):
             feats = pl.ds(zb * 384, 384)
@@ -286,8 +283,7 @@
         dst[...] = (a[...].astype(F32) + b[...].astype(F32)).astype(BF16)
 
     def pair_copy(c):
-        n = PAIR_FIRST.index(c)
-        return remote(q.at[c, :, 1 - y], yq.at[n], q_ss.at[c, 0], q_rs.at[c, 0], y_pair)
+        return remote(q.at[c, :, 1 - y], yq.at[c // 2], q_ss.at[c, 0], q_rs.at[c, 0], y_pair)
 
     def pair_ring1(c):
         return (
@@ -324,60 +320,63 @@
         for copy in copies:
             copy.start()
 
-    def step_a(c):
-        hidden_chunk(c)
-        start((pair_copy(c),) if c in PAIR_FIRST else ring1(c))
-
-    def step_b(c):
-        if c in PAIR_FIRST:
-            pair_copy(c).wait_recv()
-            for zb in range(4):
-                blk = q.at[c, zb, y]
-                add_into(blk, blk, yq.at[PAIR_FIRST.index(c), zb])
-            start(pair_ring1(c))
-        else:
-            first, second = ring1(c)[:2]
-            first.wait_recv()
-            add_into(q.at[c, zp, 0], q.at[c, zp, 0], ra.at[c])
-            second.wait_recv()
-            add_into(q.at[c, zn, 1], q.at[c, zn, 1], rb.at[c])
-            start(ring2(c))
-
-    def step_c(c):
-        if c in PAIR_FIRST:
-            first, second = pair_ring1(c)[:2]
-            first.wait_recv()
-            add_into(q.at[c, zp, y, lo], q.at[c, zp, y, lo], ra.at[c, lo])
-            second.wait_recv()
-            add_into(q.at[c, zn, y, hi], q.at[c, zn, y, hi], rb.at[c, lo])
-            start(pair_ring2(c))
-        else:
-            for copy in ring1(c)[2:] + ring2(c):
-                copy.wait_recv()
-            for half in range(2):
-                blk = q.at[c, z, half]
-                blk[...] = (
-                    blk[...].astype(F32) + sa[c, half].astype(F32) + sb[c, half].astype(F32)
-                ).astype(BF16)
-            ring_pair(c).start()
+    def pair_b(c):
+        pair_copy(c).wait_recv()
+
+        @pl.loop(0, 4)
+        def _(zb):
+            blk = q.at[c, zb, y]
+            add_into(blk, blk, yq.at[c // 2, zb])
+
+        start(pair_ring1(c))
+
+    def ring_b(c):
+        first, second = ring1(c)[:2]
+        first.wait_recv()
+        add_into(q.at[c, zp, 0], q.at[c, zp, 0], ra.at[c])
+        second.wait_recv()
+        add_into(q.at[c, zn, 1], q.at[c, zn, 1], rb.at[c])
+        start(ring2(c))
+
+    def pair_c(c):
+        first, second = pair_ring1(c)[:2]
+        first.wait_recv()
+        add_into(q.at[c, zp, y, lo], q.at[c, zp, y, lo], ra.at[c, lo])
+        second.wait_recv()
+        add_into(q.at[c, zn, y, hi], q.at[c, zn, y, hi], rb.at[c, lo])
+        start(pair_ring2(c))
+
+    def ring_c(c):
+        for copy in ring1(c)[2:] + ring2(c):
+            copy.wait_recv()
+
+        @pl.loop(0, 2)
+        def _(half):
+            blk = q.at[c, z, half]
+            blk[...] = (
+                blk[...].astype(F32) + sa[c, half].astype(F32) + sb[c, half].astype(F32)
+            ).astype(BF16)
+
+        ring_pair(c).start()
 
     def out_copy(c):
-        rows = pl.ds(c * TOKS, TOKS)
+        rows = chunk_rows(c)
         return pltpu.make_async_copy(out.at[:, rows], out_hbm.at[:, rows], out_sem.at[c])
 
-    def step_d(c):
-        if c in PAIR_FIRST:
-            for copy in pair_ring1(c)[2:] + pair_ring2(c):
-                copy.wait_recv()
-            total = q[c, z, y].astype(F32) + sa[c, 0].astype(F32) + sb[c, 0].astype(F32)
-        else:
-            ring_pair(c).wait_recv()
-            total = q[c, z, y].astype(F32) + yr[c].astype(F32)
-        rows = pl.ds(c * TOKS, TOKS)
-        out[:, rows] = (
-            inv_t[pl.ds(c, 1), :] * total + eg_t[0:192, c:c + 1]
-        ).astype(BF16)
+    def finish(c, total):
+        lane = lax.broadcasted_iota(jnp.int32, (192, 128), 1)
+        col = jnp.sum(jnp.where(lane == c, eg_t[0:192, :], 0.0), axis=1, keepdims=True)
+        out[:, chunk_rows(c)] = (inv_t[pl.ds(c, 1), :] * total + col).astype(BF16)
         out_copy(c).start()
+
+    def pair_d(c):
+        for copy in pair_ring1(c)[2:] + pair_ring2(c):
+            copy.wait_recv()
+        finish(c, q[c, z, y].astype(F32) + sa[c, 0].astype(F32) + sb[c, 0].astype(F32))
+
+    def ring_d(c):
+        ring_pair(c).wait_recv()
+        finish(c, q[c, z, y].astype(F32) + yr[c].astype(F32))
 
     xp, xn, xo = (x + 1) % 4, (x + 3) % 4, (x + 2) % 4
     right, left = mesh_x(1), mesh_x(3)
@@ -468,101 +467,153 @@
         eg_t[...] = square.T
 
     w_in_copy.wait()
-    for c in range(0, 4):
-        tok_copy(c).wait()
     csum[...] = dot(jnp.full((16, D), 1.0, BF16), w_in[...])[0:1]
     pl.semaphore_wait(barrier, 15)
     gather_first(texts, text_ss, text_rs)
-    forward(*GROUPS[0])
-    w_out_copy.wait()
-    exchange_start(0)
-    gather_relay(texts, text_ss, text_rs)
-    for c in range(*GROUPS[0]):
-        flip(c)
-    exchange_wait(0)
-    gather_rest(texts, text_ss, text_rs)
-    loss(0)
-    for c in range(*GROUPS[0]):
-        step_a(c)
-
-    for c in range(4, CHUNKS):
-        tok_copy(c).wait()
-    forward(*GROUPS[1])
-    exchange_start(1)
-    step_b(0)
-    for c in range(*GROUPS[1]):
-        flip(c)
-    step_b(1)
-    exchange_wait(1)
-    loss(1)
-    step_b(2)
-    step_a(4)
+
+    def is_pair(c):
+        return (c % 2 == 1) & (c < 6)
+
+    @pl.loop(0, GROUPS)
+    def _(n):
+        @pl.loop(0, PER)
+        def _(p):
+            c = n * PER + p
+            tok_copy(c).wait()
+            forward(c)
+
+        @pl.when(n == 0)
+        def _():
+            w_out_copy.wait()
+
+        exchange_start(n)
+
+        @pl.when(n == 0)
+        def _():
+            gather_relay(texts, text_ss, text_rs)
+
+        @pl.when(n == 1)
+        def _():
+            @pl.loop(0, 2)
+            def _(k):
+                ring_b(2 * k)
+
+        @pl.loop(0, PER)
+        def _(p):
+            flip(n * PER + p)
+
+        @pl.when(n == 1)
+        def _():
+            pair_b(1)
+
+        exchange_wait(n)
+
+        @pl.when(n == 0)
+        def _():
+            gather_rest(texts, text_ss, text_rs)
+
+        loss(n)
+
+        @pl.when(n == 1)
+        def _():
+            pair_b(3)
+
+        @pl.loop(0, PER)
+        def _(p):
+            c = n * PER + p
+            hidden_chunk(c)
+
+            @pl.when(is_pair(c))
+            def _():
+                pair_copy(c).start()
+
+            @pl.when(jnp.logical_not(is_pair(c)))
+            def _():
+                start(ring1(c))
+
+            @pl.when((n == 1) & (p < 2))
+            def _():
+                ring_c(2 * p)
+
+            @pl.when((n == 1) & (p >= 2))
+            def _():
+                pair_c(2 * p - 3)
+
+    def late_ring(k):
+        return jnp.minimum(4 + 2 * k, 7)
+
     gather_first(msgs, msg_ss, msg_rs)
-    step_c(0)
-    step_a(5)
-    step_b(3)
-    step_a(6)
-    step_c(2)
-    step_a(7)
-    step_c(1)
     own_columns()
     weight_a()
+
+    @pl.loop(0, 3)
+    def _(k):
+        ring_b(late_ring(k))
+
+    weight_b()
+    pair_b(5)
+
+    @pl.loop(0, 2)
+    def _(k):
+        ring_d(2 * k)
+
     gather_relay(msgs, msg_ss, msg_rs)
-    step_b(4)
-    step_c(3)
-    weight_b()
-    step_d(0)
-    step_b(6)
-    step_b(7)
-    step_b(5)
-    step_d(2)
     weight_c()
+
+    @pl.loop(0, 2)
+    def _(k):
+        pair_d(2 * k + 1)
+
     gathered()
-    step_c(4)
-    step_d(1)
-    step_d(3)
+    pair_c(5)
+
+    @pl.loop(0, 3)
+    def _(k):
+        ring_c(late_ring(k))
+
     weight_d()
-    step_c(6)
-    step_c(7)
-    step_c(5)
-    step_d(4)
+    pair_d(5)
+
+    @pl.loop(0, 3)
+    def _(k):
+        ring_d(late_ring(k))
+
     weight_e()
-    step_d(6)
-    step_d(7)
-    step_d(5)
-
-    for c in range(CHUNKS):
-        if c in PAIR_FIRST:
-            copies = (pair_copy(c),) + pair_ring1(c) + pair_ring2(c)
-        else:
-            copies = (ring_pair(c),) + ring1(c) + ring2(c)
-        for copy in copies:
-            copy.wait_send()
+
+    @pl.loop(0, CHUNKS)
+    def _(c):
+        out_copy(c).wait()
+
+        @pl.when(is_pair(c))
+        def _():
+            for copy in (pair_copy(c),) + pair_ring1(c) + pair_ring2(c):
+                copy.wait_send()
+
+        @pl.when(jnp.logical_not(is_pair(c)))
+        def _():
+            for copy in (ring_pair(c),) + ring1(c) + ring2(c):
+                copy.wait_send()
+
     for copy in (core_copy, g1a, g1b, g2a, g2b, g3):
         copy.wait_send()
-    for n in range(len(GROUPS)):
-        @pl.loop(1, 8)
-        def _(k):
+
+    @pl.loop(1, 8)
+    def _(k):
+        for n in range(GROUPS):
             emb_copy(n, k).wait_send()
 
     gather_sent(texts, text_ss, text_rs)
     gather_sent(msgs, msg_ss, msg_rs)
-    for c in range(CHUNKS):
-        out_copy(c).wait()
     small_out(win, win_hbm, 0).wait()
     small_out(tgrad, tgrad_hbm, 1).wait()
     small_out(wout, wout_hbm, 2).wait()
 
 
-def hand_out(a, b, c, d, a_out, b_out, c_out, d_out, sem):
-    copies = [
-        pltpu.make_async_copy(src, dst, sem.at[k])
-        for k, (src, dst) in enumerate(((a, a_out), (b, b_out), (c, c_out), (d, d_out)))
-    ]
-    for copy in copies:
-        copy.start()
-    for copy in copies:
-        copy.wait()
+def hand_out(a, b, c, d, a_out, b_out, c_out, d_out):
+    a_out[...] = a[...]
+    b_out[...] = b[...]
+    c_out[...] = c[...]
+    d_out[...] = d[...]
 
 
 def body(tokens, w_in, w_out, text_emb, labels, logit_scale, logit_bias):
@@ -570,7 +621,6 @@
     smem = pl.BlockSpec(memory_space=pltpu.SMEM)
     hbm = pl.BlockSpec(memory_space=pl.ANY)
     msg = D + HID + 256
-    groups = len(GROUPS)
     scratch = [
         pltpu.VMEM((ROWS, D), BF16),
         pltpu.VMEM((ROWS, 1), F32),
@@ -589,7 +639,7 @@
         pltpu.VMEM((256, 128), F32),
         pltpu.VMEM((256, HALF), F32),
         pltpu.VMEM((16, 16, HALF), BF16),
-        pltpu.VMEM((groups, 8, 16, HALF), BF16),
+        pltpu.VMEM((GROUPS, 8, 16, HALF), BF16),
         pltpu.VMEM((16, 16, msg), BF16),
         pltpu.VMEM((CHUNKS, 4, 2, 192, TOKS), BF16),
         pltpu.VMEM((CHUNKS, 192, TOKS), BF16),
@@ -597,7 +647,7 @@
         pltpu.VMEM((CHUNKS, 2, 192, TOKS), BF16),
         pltpu.VMEM((CHUNKS, 2, 192, TOKS), BF16),
         pltpu.VMEM((CHUNKS, 192, TOKS), BF16),
-        pltpu.VMEM((len(PAIR_FIRST), 4, 192, TOKS), BF16),
+        pltpu.VMEM((PAIR_FIRST, 4, 192, TOKS), BF16),
         pltpu.VMEM((4, 2, 2, 96, HID), BF16),
         pltpu.VMEM((4, 2, 96, HID), BF16),
         pltpu.VMEM((4, 2, 96, HID), BF16),
@@ -614,8 +664,8 @@
         pltpu.SemaphoreType.DMA((2,)),
         pltpu.SemaphoreType.DMA((2, 8)),
         pltpu.SemaphoreType.DMA((16,)),
-        pltpu.SemaphoreType.DMA((groups, 8)),
-        pltpu.SemaphoreType.DMA((groups, 8)),
+        pltpu.SemaphoreType.DMA((GROUPS, 8)),
+        pltpu.SemaphoreType.DMA((GROUPS, 8)),
         pltpu.SemaphoreType.DMA((2, 8)),
         pltpu.SemaphoreType.DMA((16,)),
         pltpu.SemaphoreType.DMA((CHUNKS, 7)),
@@ -646,9 +696,8 @@
     token_t, w_in_grad, w_out_t, text_grad = pl.pallas_call(
         hand_out,
         out_shape=shapes,
-        in_specs=[hbm, hbm, hbm, hbm],
-        out_specs=(hbm, hbm, hbm, hbm),
-        scratch_shapes=[pltpu.SemaphoreType.DMA((4,))],
+        in_specs=[vmem, vmem, vmem, vmem],
+        out_specs=(vmem, vmem, vmem, vmem),
         compiler_params=pltpu.CompilerParams(vmem_limit_bytes=61 * 2**20),
         cost_estimate=pl.CostEstimate(flops=0, bytes_accessed=2 * 2**20, transcendentals=0),
     )(*results)

time: 126 us -> 96.9 us (0.77)
  Pallas kernels: 122 us -> 93.1 us
    pallas_call x1, Pallas kernels: 34.6 us -> 2.21 us  [body(): pl.pallas_call(hand_out, out_shape=shapes, in_specs=[vmem, vmem, vmem, vm...]
    pallas_call x1, Pallas kernels: 87.7 us -> 90.9 us  [body(): pl.pallas_call(kernel, out_shape=shapes, in_specs=[hbm, hbm, hbm, vmem, s...]
where the time goes in v3:
time: 96.9 us; the launch traced here: 95.1 us
  Pallas kernels  93.1 us (96%)
  between operations  1.93 us (2%)
    pallas_call x1, Pallas kernels, body(): pl.pallas_call(kernel, out_shape=shapes, in_specs=[hbm, hbm, hbm, vmem, s...  90.9 us
    pallas_call x1, Pallas kernels, body(): pl.pallas_call(hand_out, out_shape=shapes, in_specs=[vmem, vmem, vmem, vm...  2.21 us

profile of v3, /device:TPU:0, one launch (start us, length us, event | category | flops | bytes accessed | tf_op | source)
XLA Modules:
  0.0 95.1 jit_solution(14673280536497000485)
XLA Ops:
  1.9 90.9 %shard_map.102 = (bf16[192,2048]{1,0:T(8,128)(2,1)}, bf16[96,768]{1,0:T(8,128)(2,1)}, bf16[96,768]{1,0:T(8,128)(2,1)}, bf16[8,1536]{1,0:T(8,128)(2,1)}) custom-call(bf16[2048,1536]{1,0:T(8,128)(2,1)} %tokens_hbm.1, bf16[1536,768]{1,0:T(8,128)(2,1)} %w_in_hbm.1, bf16[768,1536]{1,0:T(8,128)(2,1)} %w_out_hbm.1, bf16[8,1536]{1,0:T(8,128)(2,1)} %text_ref.1, ...), custom_call_target="tpu_custom_call" | custom-call | flops 14495514624 | bytes 14680064 | tf_op jit(solution)/shard_map/pallas_call | solution.py:683
  92.8 2.2 %shard_map.103 = (bf16[192,2048]{1,0:T(8,128)(2,1)}, bf16[96,768]{1,0:T(8,128)(2,1)}, bf16[96,768]{1,0:T(8,128)(2,1)}, bf16[8,1536]{1,0:T(8,128)(2,1)}) custom-call(bf16[192,2048]{1,0:T(8,128)(2,1)} %get-tuple-element.12.a, bf16[96,768]{1,0:T(8,128)(2,1)} %get-tuple-element.13.b, bf16[96,768]{1,0:T(8,128)(2,1)} %get-tuple-element.14.c, ...), custom_call_target="tpu_custom_call" | custom-call | bytes 2097152 | tf_op jit(solution)/shard_map/pallas_call | solution.py:696

commit v4 on v3

--- a/solution.py
+++ b/solution.py
@@ -38,8 +38,8 @@
 def kernel(
     tokens_hbm, w_in_hbm, w_out_hbm, text_ref, labels_ref, scale_ref, bias_ref,
     out_hbm, win_hbm, wout_hbm, tgrad_hbm,
-    tok, inv, minv, hpre, hg, nt, w_in, w_out,
-    tmean, pooled, pgs, egs, csum, inv_t, eg_t, tdir,
+    tok, inv, hpre, hs, cur, nxt, tok_t, w_in, w_out,
+    tmean, pooled, pgs, egs, csum, sums, inv_t, shift_t, eg_t, tdir,
     texts, ebuf, msgs,
     q, ra, rb, sa, sb, yr, yq,
     g, gc, gx, gra, grb, gsa, gsb, gyr,
@@ -64,9 +64,6 @@
     core_pair = (dp - core + (1 - core), tp)
     y_far = ((1 - yh) * 8 + local, tp)
 
-    def octet(k):
-        return (yh * 8 + (local + k) % 8, tp)
-
     def remote(src, dst, ssem, rsem, dev):
         return pltpu.make_async_remote_copy(
             src_ref=src, dst_ref=dst, send_sem=ssem, recv_sem=rsem,
@@ -77,13 +74,15 @@
         rows = pl.ds(c * TOKS, TOKS)
         return pltpu.make_async_copy(tokens_hbm.at[rows], tok.at[rows], tok_sem.at[c])
 
+    def w_in_copy(k):
+        feats = pl.ds(k * 256, 256)
+        return pltpu.make_async_copy(w_in_hbm.at[feats], w_in.at[feats], w_sem.at[k])
+
+    w_out_copy = pltpu.make_async_copy(w_out_hbm, w_out, w_sem.at[6])
     tok_copy(0).start()
-    w_in_copy = pltpu.make_async_copy(w_in_hbm, w_in, w_sem.at[0])
-    w_out_copy = pltpu.make_async_copy(w_out_hbm, w_out, w_sem.at[1])
-    w_in_copy.start()
-    for c in range(1, CHUNKS):
-        tok_copy(c).start()
-    w_out_copy.start()
+    for k in range(6):
+        w_in_copy(k).start()
+    tok_copy(1).start()
 
     barrier = pltpu.get_barrier_semaphore()
 
@@ -91,59 +90,70 @@
         pl.semaphore_signal(barrier, inc=1, device_id=dev, device_id_type=pl.DeviceIdType.MESH)
 
     greet(y_far)
+    greet(core_pair)
+    for k in range(1, 4):
+        greet(mesh_x(k))
     for k in range(1, 8):
-        greet(octet(k))
         greet((dp, (tp + k) % 8))
 
+    mine, far = yh * 4 + x, (1 - yh) * 4 + x
     text_vals = text_ref[...].astype(F32)
     text_inv = lax.rsqrt(jnp.sum(text_vals * text_vals, axis=1, keepdims=True) + EPS)
     text_nrm = text_vals * text_inv
-    texts[dp] = jnp.concatenate([text_nrm[:, :HALF], text_nrm[:, HALF:]], axis=0).astype(BF16)
+    texts[core, mine] = jnp.concatenate([text_nrm[:, :HALF], text_nrm[:, HALF:]], axis=0).astype(BF16)
     tmean[...] = jnp.zeros_like(tmean)
     pooled[...] = jnp.zeros_like(pooled)
 
-    def gather_send(buf, slot, ss, rs, row):
-        @pl.loop(1, 8)
-        def _(k):
-            remote(buf.at[slot], buf.at[slot], ss.at[row, k], rs.at[slot], octet(k)).start()
-
     def gather_far(buf, ss, rs):
-        return remote(buf.at[dp], buf.at[dp], ss.at[0, 0], rs.at[dp], y_far)
-
-    def gather_recv(buf, slot, ss, rs):
-        remote(buf.at[slot], buf.at[slot], ss.at[0, 0], rs.at[slot], y_far).wait_recv()
+        return remote(buf.at[core, mine], buf.at[core, mine], ss.at[0], rs.at[mine], y_far)
+
+    def gather_x(buf, slot, k, ss, rs, first):
+        block = buf.at[core, slot]
+        return remote(block, block, ss.at[first + k], rs.at[slot], mesh_x(k))
+
+    def gather_core(buf, ss, rs):
+        return remote(buf.at[core], buf.at[core], ss.at[7], rs.at[8], core_pair)
 
     def gather_first(buf, ss, rs):
         gather_far(buf, ss, rs).start()
-        gather_send(buf, dp, ss, rs, 0)
-
-    far_slot = (1 - yh) * 8 + local
+        for k in range(1, 4):
+            gather_x(buf, mine, k, ss, rs, 0).start()
 
     def gather_relay(buf, ss, rs):
-        gather_recv(buf, far_slot, ss, rs)
-        gather_send(buf, far_slot, ss, rs, 1)
+        gather_x(buf, far, 1, ss, rs, 3).wait_recv()
+        for k in range(1, 4):
+            gather_x(buf, far, k, ss, rs, 3).start()
+
+    def gather_pass(buf, ss, rs):
+        for k in range(1, 4):
+            for side in range(2):
+                gather_x(buf, side * 4 + (x + k) % 4, k, ss, rs, 0).wait_recv()
+        gather_core(buf, ss, rs).start()
 
     def gather_rest(buf, ss, rs):
-        @pl.loop(1, 8)
-        def _(k):
-            gather_recv(buf, yh * 8 + (local + k) % 8, ss, rs)
-            gather_recv(buf, (1 - yh) * 8 + (local + k) % 8, ss, rs)
+        remote(buf.at[1 - core], buf.at[1 - core], ss.at[7], rs.at[8], core_pair).wait_recv()
 
     def gather_sent(buf, ss, rs):
         gather_far(buf, ss, rs).wait_send()
-
-        @pl.loop(1, 8)
-        def _(k):
-            for row in range(2):
-                remote(buf.at[dp], buf.at[dp], ss.at[row, k], rs.at[dp], octet(k)).wait_send()
+        for k in range(1, 4):
+            gather_x(buf, mine, k, ss, rs, 0).wait_send()
+            gather_x(buf, far, k, ss, rs, 3).wait_send()
+        gather_core(buf, ss, rs).wait_send()
+
+    def split(vals):
+        top = vals.astype(BF16).astype(F32)
+        return jnp.concatenate(
+            [top, vals - top, jnp.zeros((14,) + vals.shape[1:], F32)], axis=0
+        ).astype(BF16)
 
     def chunk_rows(c):
         return pl.ds(pl.multiple_of(c * TOKS, TOKS), TOKS)
 
     def forward(c):
-        block = tok[chunk_rows(c), :]
-        accs = [dot(block, w_in[:, j * 256:(j + 1) * 256]) for j in range(3)]
-        scales, shifts = [], []
+        accs = [
+            dot(tok[chunk_rows(c), :], w_in[0:D, j * 256:(j + 1) * 256]) for j in range(3)
+        ]
+        means, scales, shifts = [], [], []
         acc = jnp.zeros((8, D), F32)
         for b in range(TOKS // 16):
             rows = pl.ds(pl.multiple_of(c * TOKS + b * 16, 16), 16)
@@ -154,10 +164,17 @@
             scale = lax.rsqrt(var + EPS)
             shift = mean * scale
             inv[rows, :] = scale
-            minv[rows, :] = shift
+            means.append(mean)
             scales.append(scale)
             shifts.append(shift)
             acc = acc + (vals[:8] + vals[8:])
+        tok_t[0:D, chunk_rows(c)] = tok[chunk_rows(c), :].T
+        lane = lax.broadcasted_iota(jnp.int32, (TOKS, 128), 1)
+        trio = jnp.where(lane == 0, jnp.concatenate(scales, 0), jnp.concatenate(shifts, 0))
+        trio = jnp.where(lane == 2, jnp.concatenate(means, 0), trio).T
+        inv_t[pl.ds(c, 1), :] = trio[0:1, :]
+        shift_t[pl.ds(c, 1), :] = trio[1:2, :]
+        tok_t[D:D + 16, chunk_rows(c)] = split(trio[2:3, :])
         tmean[pl.ds(c, 1), :] = jnp.sum(acc, axis=0, keepdims=True) * (1.0 / TOKS)
         for j in range(3):
             cols = slice(j * 256, (j + 1) * 256)
@@ -193,13 +210,6 @@
                 ebuf.at[n, src], ebuf.at[n, src], emb_ss.at[n, k], emb_rs.at[n, src], (dp, src)
             ).wait_recv()
 
-    def flip(c):
-        rows = chunk_rows(c)
-        scale = inv[rows, :]
-        normed = (tok[rows, :].astype(F32) * scale - minv[rows, :]).astype(BF16)
-        nt[:, rows] = normed.T
-        inv_t[pl.ds(c, 1), :] = jnp.broadcast_to(scale, (TOKS, 128)).T[0:1, :]
-
     def both(sums):
         total = sums[:IMGS] + sums[IMGS:]
         return jnp.concatenate([total, total], axis=0)
@@ -219,7 +229,8 @@
         lane = lax.broadcasted_iota(jnp.int32, (IMGS, 256), 1)
         row = lax.broadcasted_iota(jnp.int32, (IMGS, 256), 0)
         valid = (lane % 16) < 8
-        text_id = (lane // 16) * 8 + lane % 16
+        slot = lane // 16
+        text_id = ((slot // 4) % 2 * 8 + slot % 4 * 2 + slot // 8) * 8 + lane % 16
         label = jnp.zeros((IMGS, 256), jnp.int32)
         for k in range(IMGS):
             label = jnp.where(row == k, labels_ref[k], label)
@@ -236,44 +247,42 @@
             dot(eg_bf[:IMGS], w_out[:, :HALF], NT) + dot(eg_bf[IMGS:], w_out[:, HALF:], NT)
         ) * (1.0 / TOKS)
         egs[...] = emb_grad * (1.0 / TOKS)
-        msgs[dp, :, 0:HALF] = image_bf
-        msgs[dp, :, HALF:D] = eg_bf
+        msgs[core, mine, :, 0:HALF] = image_bf
+        msgs[core, mine, :, HALF:D] = eg_bf
         pooled_f = pooled[...]
-        msgs[dp, :, D:D + HID] = jnp.concatenate([pooled_f, pooled_f], axis=0).astype(BF16)
-        msgs[dp, :, D + HID:D + HID + 256] = grad
-
-    def hidden_chunk(c):
-        pg = pgs[pl.ds(c, 1), :]
-        cs = csum[...]
-        first, second = [], []
+        msgs[core, mine, :, D:D + HID] = jnp.concatenate([pooled_f, pooled_f], axis=0).astype(BF16)
+        msgs[core, mine, :, D + HID:D + HID + 256] = grad
+
+    def hidden_rows(c):
+        half_pg = 0.5 * pgs[pl.ds(c, 1), :]
+        second = []
         for b in range(TOKS // 16):
             rows = pl.ds(pl.multiple_of(c * TOKS + b * 16, 16), 16)
             h = hpre[rows, :]
             h2 = h * h
             t = jnp.tanh(h * (GELU_A + (GELU_A * GELU_B) * h2))
             slope = (1.0 + t) + h * (1.0 - t * t) * (GELU_A + (3.0 * GELU_A * GELU_B) * h2)
-            grad_bf = (slope * (0.5 * pg)).astype(BF16)
-            hg[rows, :] = grad_bf
-            grad_h = grad_bf.astype(F32)
-            p1 = grad_h * cs
-            p2 = grad_h * h
-            s1 = p1[:, 0:128]
+            grad_bf = (slope * half_pg * inv[rows, :]).astype(BF16)
+            hs[rows, :] = grad_bf
+            nxt[b * 16:(b + 1) * 16, :] = grad_bf
+            p2 = grad_bf.astype(F32) * h
             s2 = p2[:, 0:128]
             for i in range(1, HID // 128):
-                s1 = s1 + p1[:, i * 128:(i + 1) * 128]
                 s2 = s2 + p2[:, i * 128:(i + 1) * 128]
-            first.append(s1)
             second.append(s2)
-        m1 = jnp.sum(jnp.concatenate(first, axis=0).T, axis=0, keepdims=True) * (1.0 / D)
         m2 = jnp.sum(jnp.concatenate(second, axis=0).T, axis=0, keepdims=True) * (1.0 / D)
+        sums[0:1, :] = inv_t[pl.ds(c, 1), :] * m2
+        sums[1:2, :] = shift_t[pl.ds(c, 1), :] * m2
+
+    def feature_rows(c):
         rows = chunk_rows(c)
-        hgc = hg[rows, :]
-        for zb in range(4):
-            feats = pl.ds(zb * 384, 384)
-            block = dot(w_in[feats, :], hgc, NT) - m1 - nt[feats, rows].astype(F32) * m2
-            block = block.astype(BF16)
-            q[c, zb, 0] = block[:192]
-            q[c, zb, 1] = block[192:]
+        full = dot(w_in[...], cur[...], NT)
+        slope = sums[0:1, :]
+        shift = (full[D:D + 1] + full[D + 1:D + 2]) * (1.0 / D) - sums[1:2, :]
+        for k in range(8):
+            feats = slice(k * 192, (k + 1) * 192)
+            block = full[feats] - tok_t[feats, rows].astype(F32) * slope - shift
+            q[c, k // 2, k % 2] = block.astype(BF16)
 
     zp, zn, zo = (z + 1) % 4, (z + 3) % 4, (z + 2) % 4
     up, down = mesh_z(1), mesh_z(3)
@@ -366,7 +375,7 @@
     def finish(c, total):
         lane = lax.broadcasted_iota(jnp.int32, (192, 128), 1)
         col = jnp.sum(jnp.where(lane == c, eg_t[0:192, :], 0.0), axis=1, keepdims=True)
-        out[:, chunk_rows(c)] = (inv_t[pl.ds(c, 1), :] * total + col).astype(BF16)
+        out[:, chunk_rows(c)] = (total + col).astype(BF16)
         out_copy(c).start()
 
     def pair_d(c):
@@ -381,66 +390,76 @@
     xp, xn, xo = (x + 1) % 4, (x + 3) % 4, (x + 2) % 4
     right, left = mesh_x(1), mesh_x(3)
 
-    core_copy = remote(g.at[:, :, 1 - core], gc, g_ss.at[0], g_rs.at[0], core_pair)
-    g1a = remote(gx.at[xo, 0], gra, g_ss.at[1], g_rs.at[1], right)
-    g1b = remote(gx.at[xo, 1], grb, g_ss.at[2], g_rs.at[2], left)
-    g2a = remote(gx.at[xp], gsa, g_ss.at[3], g_rs.at[3], right)
-    g2b = remote(gx.at[xn], gsb, g_ss.at[4], g_rs.at[4], left)
-    g3 = remote(gx.at[x, 1 - yh], gyr, g_ss.at[5], g_rs.at[5], y_far)
-
-    def weight_a():
-        @pl.loop(0, 4)
-        def _(i):
-            feats = pl.ds(pl.multiple_of(i * 384, 384), 384)
-            block = dot(nt[feats, :], hg[...]).astype(BF16)
-            for k in range(4):
-                g[i, k // 2, k % 2] = block[k * 96:(k + 1) * 96]
-
-        core_copy.start()
-
-    def weight_b():
-        core_copy.wait_recv()
+    def core_copy(j):
+        return remote(g.at[j, :, :, 1 - core], gc.at[j], g_ss.at[j, 0], g_rs.at[j, 0], core_pair)
+
+    def g1(j):
+        return (
+            remote(gx.at[j, xo, 0], gra.at[j], g_ss.at[j, 1], g_rs.at[j, 1], right),
+            remote(gx.at[j, xo, 1], grb.at[j], g_ss.at[j, 2], g_rs.at[j, 2], left),
+        )
+
+    def g2(j):
+        return (
+            remote(gx.at[j, xp], gsa.at[j], g_ss.at[j, 3], g_rs.at[j, 3], right),
+            remote(gx.at[j, xn], gsb.at[j], g_ss.at[j, 4], g_rs.at[j, 4], left),
+        )
+
+    def g3(j):
+        return remote(gx.at[j, x, 1 - yh], gyr.at[j], g_ss.at[j, 5], g_rs.at[j, 5], y_far)
+
+    def weight_a(j):
+        cols = pl.ds(pl.multiple_of(j * 256, 256), 256)
+        full = dot(tok_t[...], hs[:, cols])
+        lift = full[D:D + 1] + full[D + 1:D + 2]
+        g[j] = (full[:D] - lift).astype(BF16).reshape(4, 2, 2, 96, 256)
+        core_copy(j).start()
+
+    def weight_b(j):
+        core_copy(j).wait_recv()
 
         @pl.loop(0, 8)
         def _(k):
             xb, yb = k // 2, k % 2
-            i, j = yb * 2 + xb // 2, xb % 2
-            add_into(gx.at[xb, yb], g.at[i, j, core], gc.at[i, j])
-
-        g1a.start()
-        g1b.start()
-
-    def weight_c():
-        g1a.wait_recv()
-        add_into(gx.at[xp, 0], gx.at[xp, 0], gra)
-        g1b.wait_recv()
-        add_into(gx.at[xn, 1], gx.at[xn, 1], grb)
-        g2a.start()
-        g2b.start()
-
-    def weight_d():
-        g2a.wait_recv()
-        g2b.wait_recv()
+            i, m = yb * 2 + xb // 2, xb % 2
+            add_into(gx.at[j, xb, yb], g.at[j, i, m, core], gc.at[j, i, m])
+
+        start(g1(j))
+
+    def weight_c(j):
+        first, second = g1(j)
+        first.wait_recv()
+        add_into(gx.at[j, xp, 0], gx.at[j, xp, 0], gra.at[j])
+        second.wait_recv()
+        add_into(gx.at[j, xn, 1], gx.at[j, xn, 1], grb.at[j])
+        start(g2(j))
+
+    def weight_d(j):
+        for copy in g2(j):
+            copy.wait_recv()
         for half in range(2):
-            blk = gx.at[x, half]
+            blk = gx.at[j, x, half]
             blk[...] = (
-                blk[...].astype(F32) + gsa[half].astype(F32) + gsb[half].astype(F32)
+                blk[...].astype(F32) + gsa[j, half].astype(F32) + gsb[j, half].astype(F32)
             ).astype(BF16)
-        g3.start()
+        g3(j).start()
+
+    def weight_e():
+        for j in range(3):
+            g3(j).wait_recv()
+            win[:, j * 256:(j + 1) * 256] = (
+                gx[j, x, yh].astype(F32) + gyr[j].astype(F32)
+            ).astype(BF16)
+        small_out(win, win_hbm, 0).start()
 
     def small_out(src, dst, k):
         return pltpu.make_async_copy(src, dst, out_sem.at[CHUNKS + k])
-
-    def weight_e():
-        g3.wait_recv()
-        win[...] = (gx[x, yh].astype(F32) + gyr[...].astype(F32)).astype(BF16)
-        small_out(win, win_hbm, 0).start()
 
     def gathered():
         gather_rest(msgs, msg_ss, msg_rs)
         all_msgs = msgs[...].reshape(256, D + HID + 256)
         tdir[...] = dot(all_msgs[:, D + HID:], all_msgs[:, :HALF], TN)
-        text_dir = scale * tdir[pl.ds(pl.multiple_of(dp * 16, 16), 16), :]
+        text_dir = scale * tdir[pl.ds(pl.multiple_of((core * 8 + mine) * 16, 16), 16), :]
         text_dir = jnp.concatenate([text_dir[:IMGS], text_dir[IMGS:]], axis=1)
         vals = text_ref[...].astype(F32)
         t_inv = lax.rsqrt(jnp.sum(vals * vals, axis=1, keepdims=True) + EPS)
@@ -466,62 +485,79 @@
         square = jnp.concatenate([square, jnp.zeros((120, 256), F32)], axis=0)
         eg_t[...] = square.T
 
-    w_in_copy.wait()
-    csum[...] = dot(jnp.full((16, D), 1.0, BF16), w_in[...])[0:1]
-    pl.semaphore_wait(barrier, 15)
+    for k in range(6):
+        w_in_copy(k).wait()
+
+    @pl.loop(2, CHUNKS)
+    def _(c):
+        tok_copy(c).start()
+
+    w_out_copy.start()
+    cs = dot(jnp.full((16, D), 1.0, BF16), w_in[0:D, :])[0:1]
+    csum[...] = cs
+    w_in[D:D + 16, :] = split(cs)
+    pl.semaphore_wait(barrier, 12)
     gather_first(texts, text_ss, text_rs)
 
     def is_pair(c):
         return (c % 2 == 1) & (c < 6)
 
+    def forward_loop(first, last):
+        @pl.loop(first, last)
+        def _(c):
+            tok_copy(c).wait()
+            forward(c)
+
     @pl.loop(0, GROUPS)
     def _(n):
+        @pl.loop(5 * n, 4 + 4 * n)
+        def _(c):
+            tok_copy(c).wait()
+            forward(c)
+
+            @pl.when(c == 6)
+            def _():
+                ring_b(2)
+
+        @pl.when(n == 0)
+        def _():
+            w_out_copy.wait()
+
+        exchange_start(n)
+
+        @pl.when(n == 0)
+        def _():
+            gather_relay(texts, text_ss, text_rs)
+            forward_loop(4, 5)
+            gather_pass(texts, text_ss, text_rs)
+
+        @pl.when(n == 1)
+        def _():
+            pair_b(1)
+            ring_c(0)
+
+        exchange_wait(n)
+
+        @pl.when(n == 0)
+        def _():
+            gather_rest(texts, text_ss, text_rs)
+
+        loss(n)
+
+        @pl.when(n == 1)
+        def _():
+            pair_c(1)
+            ring_c(2)
+            gather_first(msgs, msg_ss, msg_rs)
+
+        hidden_rows(n * PER)
+
         @pl.loop(0, PER)
         def _(p):
             c = n * PER + p
-            tok_copy(c).wait()
-            forward(c)
-
-        @pl.when(n == 0)
-        def _():
-            w_out_copy.wait()
-
-        exchange_start(n)
-
-        @pl.when(n == 0)
-        def _():
-            gather_relay(texts, text_ss, text_rs)
-
-        @pl.when(n == 1)
-        def _():
-            @pl.loop(0, 2)
-            def _(k):
-                ring_b(2 * k)
-
-        @pl.loop(0, PER)
-        def _(p):
-            flip(n * PER + p)
-
-        @pl.when(n == 1)
-        def _():
-            pair_b(1)
-
-        exchange_wait(n)
-
-        @pl.when(n == 0)
-        def _():
-            gather_rest(texts, text_ss, text_rs)
-
-        loss(n)
-
-        @pl.when(n == 1)
-        def _():
-            pair_b(3)
-
-        @pl.loop(0, PER)
-        def _(p):
-            c = n * PER + p
-            hidden_chunk(c)
+            cur[...] = nxt[...]
+            feature_rows(c)
+            hidden_rows(jnp.minimum(c + 1, n * PER + PER - 1))
 
             @pl.when(is_pair(c))
             def _():
@@ -531,53 +567,64 @@
             def _():
                 start(ring1(c))
 
-            @pl.when((n == 1) & (p < 2))
+            @pl.when(c == 3)
             def _():
-                ring_c(2 * p)
-
-            @pl.when((n == 1) & (p >= 2))
+                ring_b(0)
+
+            @pl.when(c == 5)
             def _():
-                pair_c(2 * p - 3)
-
-    def late_ring(k):
-        return jnp.minimum(4 + 2 * k, 7)
-
-    gather_first(msgs, msg_ss, msg_rs)
+                pair_b(3)
+
+            @pl.when(c == 6)
+            def _():
+                ring_b(4)
+                gather_relay(msgs, msg_ss, msg_rs)
+
+            @pl.when(c == 7)
+            def _():
+                pair_c(3)
+
     own_columns()
-    weight_a()
 
     @pl.loop(0, 3)
-    def _(k):
-        ring_b(late_ring(k))
-
-    weight_b()
-    pair_b(5)
-
-    @pl.loop(0, 2)
-    def _(k):
-        ring_d(2 * k)
-
-    gather_relay(msgs, msg_ss, msg_rs)
-    weight_c()
-
-    @pl.loop(0, 2)
-    def _(k):
-        pair_d(2 * k + 1)
-
+    def _(j):
+        weight_a(j)
+
+        @pl.when(j == 0)
+        def _():
+            ring_b(6)
+            gather_pass(msgs, msg_ss, msg_rs)
+
+        @pl.when(j == 1)
+        def _():
+            ring_b(7)
+            ring_c(4)
+            weight_b(0)
+
+        @pl.when(j == 2)
+        def _():
+            pair_b(5)
+
+    weight_b(1)
+    ring_c(6)
+    weight_c(0)
+    weight_b(2)
+    pair_c(5)
+    ring_c(7)
+    weight_c(1)
+    ring_d(0)
+    pair_d(1)
+    weight_d(0)
+    weight_c(2)
     gathered()
-    pair_c(5)
-
-    @pl.loop(0, 3)
-    def _(k):
-        ring_c(late_ring(k))
-
-    weight_d()
+    weight_d(1)
+    ring_d(2)
+    pair_d(3)
+    weight_d(2)
+    ring_d(4)
+    ring_d(6)
     pair_d(5)
-
-    @pl.loop(0, 3)
-    def _(k):
-        ring_d(late_ring(k))
-
+    ring_d(7)
     weight_e()
 
     @pl.loop(0, CHUNKS)
@@ -594,8 +641,10 @@
             for copy in (ring_pair(c),) + ring1(c) + ring2(c):
                 copy.wait_send()
 
-    for copy in (core_copy, g1a, g1b, g2a, g2b, g3):
-        copy.wait_send()
+    @pl.loop(0, 3)
+    def _(j):
+        for copy in (core_copy(j), g3(j)) + g1(j) + g2(j):
+            copy.wait_send()
 
     @pl.loop(1, 8)
     def _(k):
@@ -624,23 +673,26 @@
     scratch = [
         pltpu.VMEM((ROWS, D), BF16),
         pltpu.VMEM((ROWS, 1), F32),
-        pltpu.VMEM((ROWS, 1), F32),
         pltpu.VMEM((ROWS, HID), F32),
         pltpu.VMEM((ROWS, HID), BF16),
-        pltpu.VMEM((D, ROWS), BF16),
-        pltpu.VMEM((D, HID), BF16),
+        pltpu.VMEM((TOKS, HID), BF16),
+        pltpu.VMEM((TOKS, HID), BF16),
+        pltpu.VMEM((D + 16, ROWS), BF16),
+        pltpu.VMEM((D + 16, HID), BF16),
         pltpu.VMEM((HID, D), BF16),
         pltpu.VMEM((IMGS, D), F32),
         pltpu.VMEM((IMGS, HID), F32),
         pltpu.VMEM((IMGS, HID), F32),
         pltpu.VMEM((16, HALF), F32),
         pltpu.VMEM((1, HID), F32),
+        pltpu.VMEM((8, TOKS), F32),
+        pltpu.VMEM((CHUNKS, TOKS), F32),
         pltpu.VMEM((CHUNKS, TOKS), F32),
         pltpu.VMEM((256, 128), F32),
         pltpu.VMEM((256, HALF), F32),
-        pltpu.VMEM((16, 16, HALF), BF16),
+        pltpu.VMEM((2, 8, 16, HALF), BF16),
         pltpu.VMEM((GROUPS, 8, 16, HALF), BF16),
-        pltpu.VMEM((16, 16, msg), BF16),
+        pltpu.VMEM((2, 8, 16, msg), BF16),
         pltpu.VMEM((CHUNKS, 4, 2, 192, TOKS), BF16),
         pltpu.VMEM((CHUNKS, 192, TOKS), BF16),
         pltpu.VMEM((CHUNKS, 192, TOKS), BF16),
@@ -648,30 +700,30 @@
         pltpu.VMEM((CHUNKS, 2, 192, TOKS), BF16),
         pltpu.VMEM((CHUNKS, 192, TOKS), BF16),
         pltpu.VMEM((PAIR_FIRST, 4, 192, TOKS), BF16),
-        pltpu.VMEM((4, 2, 2, 96, HID), BF16),
-        pltpu.VMEM((4, 2, 96, HID), BF16),
-        pltpu.VMEM((4, 2, 96, HID), BF16),
-        pltpu.VMEM((96, HID), BF16),
-        pltpu.VMEM((96, HID), BF16),
-        pltpu.VMEM((2, 96, HID), BF16),
-        pltpu.VMEM((2, 96, HID), BF16),
-        pltpu.VMEM((96, HID), BF16),
+        pltpu.VMEM((3, 4, 2, 2, 96, 256), BF16),
+        pltpu.VMEM((3, 4, 2, 96, 256), BF16),
+        pltpu.VMEM((3, 4, 2, 96, 256), BF16),
+        pltpu.VMEM((3, 96, 256), BF16),
+        pltpu.VMEM((3, 96, 256), BF16),
+        pltpu.VMEM((3, 2, 96, 256), BF16),
+        pltpu.VMEM((3, 2, 96, 256), BF16),
+        pltpu.VMEM((3, 96, 256), BF16),
         pltpu.VMEM((192, ROWS), BF16),
         pltpu.VMEM((96, HID), BF16),
         pltpu.VMEM((96, HID), BF16),
         pltpu.VMEM((IMGS, D), BF16),
         pltpu.SemaphoreType.DMA((CHUNKS,)),
-        pltpu.SemaphoreType.DMA((2,)),
-        pltpu.SemaphoreType.DMA((2, 8)),
-        pltpu.SemaphoreType.DMA((16,)),
+        pltpu.SemaphoreType.DMA((7,)),
+        pltpu.SemaphoreType.DMA((8,)),
+        pltpu.SemaphoreType.DMA((9,)),
         pltpu.SemaphoreType.DMA((GROUPS, 8)),
         pltpu.SemaphoreType.DMA((GROUPS, 8)),
-        pltpu.SemaphoreType.DMA((2, 8)),
-        pltpu.SemaphoreType.DMA((16,)),
+        pltpu.SemaphoreType.DMA((8,)),
+        pltpu.SemaphoreType.DMA((9,)),
         pltpu.SemaphoreType.DMA((CHUNKS, 7)),
         pltpu.SemaphoreType.DMA((CHUNKS, 7)),
-        pltpu.SemaphoreType.DMA((6,)),
-        pltpu.SemaphoreType.DMA((6,)),
+        pltpu.SemaphoreType.DMA((3, 6)),
+        pltpu.SemaphoreType.DMA((3, 6)),
         pltpu.SemaphoreType.DMA((CHUNKS + 3,)),
     ]
     shapes = (

time: 96.9 us -> 92.5 us (0.955); the launches traced: 95.1 us -> 92.3 us
  Pallas kernels: 93.1 us -> 90.4 us
    pallas_call x1, Pallas kernels: 90.9 us -> 88.2 us  [body(): pl.pallas_call(kernel, out_shape=shapes, in_specs=[hbm, hbm, hbm, vmem, s...]
where the time goes in v4:
time: 92.5 us; the launch traced here: 92.3 us
  Pallas kernels  90.4 us (98%)
  between operations  1.93 us (2%)
    pallas_call x1, Pallas kernels, body(): pl.pallas_call(kernel, out_shape=shapes, in_specs=[hbm, hbm, hbm, vmem, s...  88.2 us
    pallas_call x1, Pallas kernels, body(): pl.pallas_call(hand_out, out_shape=shapes, in_specs=[vmem, vmem, vmem, vm...  2.21 us

profile of v4, /device:TPU:0, one launch (start us, length us, event | category | flops | bytes accessed | tf_op | source)
XLA Modules:
  0.0 92.3 jit_solution(1368009024190613203)
XLA Ops:
  1.9 88.2 %shard_map.102 = (bf16[192,2048]{1,0:T(8,128)(2,1)}, bf16[96,768]{1,0:T(8,128)(2,1)}, bf16[96,768]{1,0:T(8,128)(2,1)}, bf16[8,1536]{1,0:T(8,128)(2,1)}) custom-call(bf16[2048,1536]{1,0:T(8,128)(2,1)} %tokens_hbm.1, bf16[1536,768]{1,0:T(8,128)(2,1)} %w_in_hbm.1, bf16[768,1536]{1,0:T(8,128)(2,1)} %w_out_hbm.1, bf16[8,1536]{1,0:T(8,128)(2,1)} %text_ref.1, ...), custom_call_target="tpu_custom_call" | custom-call | flops 14495514624 | bytes 14680064 | tf_op jit(solution)/shard_map/pallas_call | solution.py:735
  90.1 2.2 %shard_map.103 = (bf16[192,2048]{1,0:T(8,128)(2,1)}, bf16[96,768]{1,0:T(8,128)(2,1)}, bf16[96,768]{1,0:T(8,128)(2,1)}, bf16[8,1536]{1,0:T(8,128)(2,1)}) custom-call(bf16[192,2048]{1,0:T(8,128)(2,1)} %get-tuple-element.12.a, bf16[96,768]{1,0:T(8,128)(2,1)} %get-tuple-element.13.b, bf16[96,768]{1,0:T(8,128)(2,1)} %get-tuple-element.14.c, ...), custom_call_target="tpu_custom_call" | custom-call | bytes 2097152 | tf_op jit(solution)/shard_map/pallas_call | solution.py:748

commit v5 on v4

--- a/solution.py
+++ b/solution.py
@@ -39,7 +39,7 @@
     tokens_hbm, w_in_hbm, w_out_hbm, text_ref, labels_ref, scale_ref, bias_ref,
     out_hbm, win_hbm, wout_hbm, tgrad_hbm,
     tok, inv, hpre, hs, cur, nxt, tok_t, w_in, w_out,
-    tmean, pooled, pgs, egs, csum, sums, inv_t, shift_t, eg_t, tdir,
+    tmean, mlp_out, pooled, pgs, egs, csum, sums, inv_t, shift_t, eg_t, tdir,
     texts, ebuf, msgs,
     q, ra, rb, sa, sb, yr, yq,
     g, gc, gx, gra, grb, gsa, gsb, gyr,
@@ -102,6 +102,7 @@
     text_nrm = text_vals * text_inv
     texts[core, mine] = jnp.concatenate([text_nrm[:, :HALF], text_nrm[:, HALF:]], axis=0).astype(BF16)
     tmean[...] = jnp.zeros_like(tmean)
+    mlp_out[...] = jnp.zeros_like(mlp_out)
     pooled[...] = jnp.zeros_like(pooled)
 
     def gather_far(buf, ss, rs):
@@ -196,7 +197,10 @@
 
     def exchange_start(n):
         part = dot(pooled[...].astype(BF16), w_out[...])
-        ebuf[n, tp] = jnp.concatenate([part[:, :HALF], part[:, HALF:]], axis=0).astype(BF16)
+        own = jnp.where(n == 0, part[:PER], part[PER:])
+        ebuf[n, tp] = jnp.concatenate(
+            [own[:, k * 384:(k + 1) * 384] for k in range(4)], axis=0
+        ).astype(BF16)
 
         @pl.loop(1, 8)
         def _(k):
@@ -218,9 +222,15 @@
 
     def loss(n):
         tm = tmean[...]
-        emb = jnp.concatenate([tm[:, :HALF], tm[:, HALF:]], axis=0)
-        for k in range(8):
-            emb = emb + ebuf[n, k].astype(F32)
+        own = ebuf[n, 0].astype(F32)
+        for k in range(1, 8):
+            own = own + ebuf[n, k].astype(F32)
+        own = jnp.concatenate([own[k * PER:(k + 1) * PER] for k in range(4)], axis=1)
+        image = lax.broadcasted_iota(jnp.int32, (IMGS, D), 0)
+        mlp = jnp.where(image // PER == n, jnp.concatenate([own, own], axis=0), mlp_out[...])
+        mlp_out[...] = mlp
+        full = tm + mlp
+        emb = jnp.concatenate([full[:, :HALF], full[:, HALF:]], axis=0)
         emb_inv = lax.rsqrt(both(jnp.sum(emb * emb, axis=1, keepdims=True)) + EPS)
         image_bf = (emb * emb_inv).astype(BF16)
         text_all = texts[...].reshape(256, HALF)
@@ -508,56 +518,54 @@
             tok_copy(c).wait()
             forward(c)
 
-    @pl.loop(0, GROUPS)
-    def _(n):
-        @pl.loop(5 * n, 4 + 4 * n)
-        def _(c):
-            tok_copy(c).wait()
-            forward(c)
-
-            @pl.when(c == 6)
-            def _():
-                ring_b(2)
-
-        @pl.when(n == 0)
+    @pl.loop(0, 3)
+    def _(stage):
+        @pl.when(stage < 2)
         def _():
-            w_out_copy.wait()
-
-        exchange_start(n)
-
-        @pl.when(n == 0)
+            @pl.loop(5 * stage, 4 + 4 * stage)
+            def _(c):
+                tok_copy(c).wait()
+                forward(c)
+
+                @pl.when(c == 5)
+                def _():
+                    ring_b(0)
+
+            @pl.when(stage == 0)
+            def _():
+                w_out_copy.wait()
+
+            exchange_start(stage)
+
+        @pl.when(stage == 0)
         def _():
             gather_relay(texts, text_ss, text_rs)
             forward_loop(4, 5)
             gather_pass(texts, text_ss, text_rs)
 
-        @pl.when(n == 1)
+        @pl.when(stage != 1)
         def _():
-            pair_b(1)
-            ring_c(0)
-
-        exchange_wait(n)
-
-        @pl.when(n == 0)
-        def _():
-            gather_rest(texts, text_ss, text_rs)
-
-        loss(n)
-
-        @pl.when(n == 1)
-        def _():
-            pair_c(1)
-            ring_c(2)
-            gather_first(msgs, msg_ss, msg_rs)
-
-        hidden_rows(n * PER)
-
-        @pl.loop(0, PER)
-        def _(p):
-            c = n * PER + p
+            n = stage // 2
+            exchange_wait(n)
+
+            @pl.when(n == 0)
+            def _():
+                gather_rest(texts, text_ss, text_rs)
+
+            loss(n)
+
+            @pl.when(n == 1)
+            def _():
+                gather_first(msgs, msg_ss, msg_rs)
+                pair_b(1)
+                ring_b(2)
+
+            hidden_rows(n * PER)
+
+        @pl.loop(2 * stage, 2 * stage + 2 + 2 * (stage // 2))
+        def _(c):
             cur[...] = nxt[...]
             feature_rows(c)
-            hidden_rows(jnp.minimum(c + 1, n * PER + PER - 1))
 
             @pl.when(is_pair(c))
             def _():
@@ -567,22 +575,24 @@
             def _():
                 start(ring1(c))
 
-            @pl.when(c == 3)
-            def _():
-                ring_b(0)
+            hidden_rows(c + 1 - (c % 4) // 3)
+
+            @pl.when(c == 2)
+            def _():
+                ring_c(0)
 
             @pl.when(c == 5)
             def _():
-                pair_b(3)
+                pair_c(1)
 
             @pl.when(c == 6)
             def _():
+                ring_c(2)
+                gather_relay(msgs, msg_ss, msg_rs)
+
+            @pl.when(c == 7)
+            def _():
                 ring_b(4)
-                gather_relay(msgs, msg_ss, msg_rs)
-
-            @pl.when(c == 7)
-            def _():
-                pair_c(3)
 
     own_columns()
 
@@ -597,35 +607,37 @@
 
         @pl.when(j == 1)
         def _():
+            pair_b(3)
+            weight_b(0)
+
+        @pl.when(j == 2)
+        def _():
             ring_b(7)
             ring_c(4)
-            weight_b(0)
-
-        @pl.when(j == 2)
-        def _():
-            pair_b(5)
 
     weight_b(1)
+    weight_c(0)
+    pair_c(3)
+    weight_b(2)
+    ring_d(0)
+    pair_d(1)
+    gathered()
+    pair_b(5)
     ring_c(6)
-    weight_c(0)
-    weight_b(2)
+    weight_c(1)
+    weight_d(0)
+    weight_c(2)
+    ring_d(2)
     pair_c(5)
     ring_c(7)
-    weight_c(1)
-    ring_d(0)
-    pair_d(1)
-    weight_d(0)
-    weight_c(2)
-    gathered()
     weight_d(1)
-    ring_d(2)
     pair_d(3)
     weight_d(2)
     ring_d(4)
     ring_d(6)
+    weight_e()
     pair_d(5)
     ring_d(7)
-    weight_e()
 
     @pl.loop(0, CHUNKS)
     def _(c):
@@ -681,6 +693,7 @@
         pltpu.VMEM((D + 16, HID), BF16),
         pltpu.VMEM((HID, D), BF16),
         pltpu.VMEM((IMGS, D), F32),
+        pltpu.VMEM((IMGS, D), F32),
         pltpu.VMEM((IMGS, HID), F32),
         pltpu.VMEM((IMGS, HID), F32),
         pltpu.VMEM((16, HALF), F32),
@@ -691,7 +704,7 @@
         pltpu.VMEM((256, 128), F32),
         pltpu.VMEM((256, HALF), F32),
         pltpu.VMEM((2, 8, 16, HALF), BF16),
-        pltpu.VMEM((GROUPS, 8, 16, HALF), BF16),
+        pltpu.VMEM((GROUPS, 8, 16, 384), BF16),
         pltpu.VMEM((2, 8, 16, msg), BF16),
         pltpu.VMEM((CHUNKS, 4, 2, 192, TOKS), BF16),
         pltpu.VMEM((CHUNKS, 192, TOKS), BF16),

time: 92.5 us -> 82.7 us (0.89)
  Pallas kernels: 90.4 us -> 80.5 us
    pallas_call x1, Pallas kernels: 88.2 us -> 78.3 us  [body(): pl.pallas_call(kernel, out_shape=shapes, in_specs=[hbm, hbm, hbm, vmem, s...]
where the time goes in v5:
time: 82.7 us; the launch traced here: 82.4 us
  Pallas kernels  80.5 us (97%)
  between operations  1.93 us (2%)
    pallas_call x1, Pallas kernels, body(): pl.pallas_call(kernel, out_shape=shapes, in_specs=[hbm, hbm, hbm, vmem, s...  78.3 us
    pallas_call x1, Pallas kernels, body(): pl.pallas_call(hand_out, out_shape=shapes, in_specs=[vmem, vmem, vmem, vm...  2.21 us

profile of v5, /device:TPU:0, one launch (start us, length us, event | category | flops | bytes accessed | tf_op | source)
XLA Modules:
  0.0 82.4 jit_solution(11210718696342264861)
XLA Ops:
  1.9 78.3 %shard_map.102 = (bf16[192,2048]{1,0:T(8,128)(2,1)}, bf16[96,768]{1,0:T(8,128)(2,1)}, bf16[96,768]{1,0:T(8,128)(2,1)}, bf16[8,1536]{1,0:T(8,128)(2,1)}) custom-call(bf16[2048,1536]{1,0:T(8,128)(2,1)} %tokens_hbm.1, bf16[1536,768]{1,0:T(8,128)(2,1)} %w_in_hbm.1, bf16[768,1536]{1,0:T(8,128)(2,1)} %w_out_hbm.1, bf16[8,1536]{1,0:T(8,128)(2,1)} %text_ref.1, ...), custom_call_target="tpu_custom_call" | custom-call | flops 14495514624 | bytes 14680064 | tf_op jit(solution)/shard_map/pallas_call | solution.py:748
  80.2 2.2 %shard_map.103 = (bf16[192,2048]{1,0:T(8,128)(2,1)}, bf16[96,768]{1,0:T(8,128)(2,1)}, bf16[96,768]{1,0:T(8,128)(2,1)}, bf16[8,1536]{1,0:T(8,128)(2,1)}) custom-call(bf16[192,2048]{1,0:T(8,128)(2,1)} %get-tuple-element.12.a, bf16[96,768]{1,0:T(8,128)(2,1)} %get-tuple-element.13.b, bf16[96,768]{1,0:T(8,128)(2,1)} %get-tuple-element.14.c, ...), custom_call_target="tpu_custom_call" | custom-call | bytes 2097152 | tf_op jit(solution)/shard_map/pallas_call | solution.py:761

commit v6 on v5

--- a/solution.py
+++ b/solution.py
@@ -518,11 +518,13 @@
             tok_copy(c).wait()
             forward(c)
 
-    @pl.loop(0, 3)
+    @pl.loop(0, 4)
     def _(stage):
-        @pl.when(stage < 2)
-        def _():
-            @pl.loop(5 * stage, 4 + 4 * stage)
+        later = (stage + 3) // 4
+
+        @pl.when(stage < 3)
+        def _():
+            @pl.loop(5 * later + stage // 2, 4 + 2 * stage)
             def _(c):
                 tok_copy(c).wait()
                 forward(c)
@@ -531,11 +533,13 @@
                 def _():
                     ring_b(0)
 
-            @pl.when(stage == 0)
-            def _():
-                w_out_copy.wait()
-
-            exchange_start(stage)
+        @pl.when(stage == 0)
+        def _():
+            w_out_copy.wait()
+
+        @pl.when(stage % 2 == 0)
+        def _():
+            exchange_start(stage // 2)
 
         @pl.when(stage == 0)
         def _():
@@ -543,9 +547,9 @@
             forward_loop(4, 5)
             gather_pass(texts, text_ss, text_rs)
 
-        @pl.when(stage != 1)
-        def _():
-            n = stage // 2
+        @pl.when(stage % 3 == 0)
+        def _():
+            n = stage // 3
             exchange_wait(n)
 
             @pl.when(n == 0)
@@ -556,13 +560,12 @@
 
             @pl.when(n == 1)
             def _():
-                gather_first(msgs, msg_ss, msg_rs)
-                pair_b(1)
-                ring_b(2)
+                pair_c(1)
+                ring_c(0)
 
             hidden_rows(n * PER)
 
-        @pl.loop(2 * stage, 2 * stage + 2 + 2 * (stage // 2))
+        @pl.loop(stage + later, stage + 2 + 3 * (stage // 3))
         def _(c):
             cur[...] = nxt[...]
             feature_rows(c)
@@ -577,17 +580,22 @@
 
             hidden_rows(c + 1 - (c % 4) // 3)
 
-            @pl.when(c == 2)
-            def _():
-                ring_c(0)
+            @pl.when(c == 3)
+            def _():
+                ring_b(2)
+                pair_b(1)
+
+            @pl.when(c == 4)
+            def _():
+                gather_first(msgs, msg_ss, msg_rs)
 
             @pl.when(c == 5)
             def _():
-                pair_c(1)
+                ring_c(2)
 
             @pl.when(c == 6)
             def _():
-                ring_c(2)
+                pair_b(3)
                 gather_relay(msgs, msg_ss, msg_rs)
 
             @pl.when(c == 7)
@@ -603,32 +611,31 @@
         @pl.when(j == 0)
         def _():
             ring_b(6)
+            pair_c(3)
             gather_pass(msgs, msg_ss, msg_rs)
 
         @pl.when(j == 1)
         def _():
-            pair_b(3)
+            ring_b(7)
             weight_b(0)
 
         @pl.when(j == 2)
         def _():
-            ring_b(7)
+            pair_b(5)
             ring_c(4)
 
     weight_b(1)
     weight_c(0)
-    pair_c(3)
     weight_b(2)
     ring_d(0)
     pair_d(1)
     gathered()
-    pair_b(5)
     ring_c(6)
     weight_c(1)
+    pair_c(5)
     weight_d(0)
     weight_c(2)
     ring_d(2)
-    pair_c(5)
     ring_c(7)
     weight_d(1)
     pair_d(3)

time: 82.7 us -> 83.4 us (level)
  no operation moved by 1% of the time
where the time goes in v6:
time: 83.4 us; the launch traced here: 83.2 us
  Pallas kernels  81.2 us (97%)
  between operations  1.93 us (2%)
    pallas_call x1, Pallas kernels, body(): pl.pallas_call(kernel, out_shape=shapes, in_specs=[hbm, hbm, hbm, vmem, s...  79 us
    pallas_call x1, Pallas kernels, body(): pl.pallas_call(hand_out, out_shape=shapes, in_specs=[vmem, vmem, vmem, vm...  2.21 us

profile of v6, /device:TPU:0, one launch (start us, length us, event | category | flops | bytes accessed | tf_op | source)
XLA Modules:
  0.0 83.2 jit_solution(16926357946644215140)
XLA Ops:
  1.9 79.0 %shard_map.102 = (bf16[192,2048]{1,0:T(8,128)(2,1)}, bf16[96,768]{1,0:T(8,128)(2,1)}, bf16[96,768]{1,0:T(8,128)(2,1)}, bf16[8,1536]{1,0:T(8,128)(2,1)}) custom-call(bf16[2048,1536]{1,0:T(8,128)(2,1)} %tokens_hbm.1, bf16[1536,768]{1,0:T(8,128)(2,1)} %w_in_hbm.1, bf16[768,1536]{1,0:T(8,128)(2,1)} %w_out_hbm.1, bf16[8,1536]{1,0:T(8,128)(2,1)} %text_ref.1, ...), custom_call_target="tpu_custom_call" | custom-call | flops 14495514624 | bytes 14680064 | tf_op jit(solution)/shard_map/pallas_call | solution.py:755
  80.9 2.2 %shard_map.103 = (bf16[192,2048]{1,0:T(8,128)(2,1)}, bf16[96,768]{1,0:T(8,128)(2,1)}, bf16[96,768]{1,0:T(8,128)(2,1)}, bf16[8,1536]{1,0:T(8,128)(2,1)}) custom-call(bf16[192,2048]{1,0:T(8,128)(2,1)} %get-tuple-element.12.a, bf16[96,768]{1,0:T(8,128)(2,1)} %get-tuple-element.13.b, bf16[96,768]{1,0:T(8,128)(2,1)} %get-tuple-element.14.c, ...), custom_call_target="tpu_custom_call" | custom-call | bytes 2097152 | tf_op jit(solution)/shard_map/pallas_call | solution.py:768

commit v7 on v5

--- a/solution.py
+++ b/solution.py
@@ -36,14 +36,14 @@
 
 
 def kernel(
-    tokens_hbm, w_in_hbm, w_out_hbm, text_ref, labels_ref, scale_ref, bias_ref,
+    tokens_hbm, w_in_hbm, w_out_hbm, text_hbm, labels_hbm, scale_ref, bias_ref,
     out_hbm, win_hbm, wout_hbm, tgrad_hbm,
     tok, inv, hpre, hs, cur, nxt, tok_t, w_in, w_out,
     tmean, mlp_out, pooled, pgs, egs, csum, sums, inv_t, shift_t, eg_t, tdir,
     texts, ebuf, msgs,
     q, ra, rb, sa, sb, yr, yq,
     g, gc, gx, gra, grb, gsa, gsb, gyr,
-    out, win, wout, tgrad,
+    out, win, wout, tgrad, text_ref, labels_ref,
     tok_sem, w_sem,
     text_ss, text_rs, emb_ss, emb_rs, msg_ss, msg_rs,
     q_ss, q_rs, g_ss, g_rs, out_sem,
@@ -79,10 +79,14 @@
         return pltpu.make_async_copy(w_in_hbm.at[feats], w_in.at[feats], w_sem.at[k])
 
     w_out_copy = pltpu.make_async_copy(w_out_hbm, w_out, w_sem.at[6])
+    text_copy = pltpu.make_async_copy(text_hbm, text_ref, w_sem.at[7])
+    labels_copy = pltpu.make_async_copy(labels_hbm, labels_ref, w_sem.at[8])
+    text_copy.start()
     tok_copy(0).start()
     for k in range(6):
         w_in_copy(k).start()
     tok_copy(1).start()
+    labels_copy.start()
 
     barrier = pltpu.get_barrier_semaphore()
 
@@ -97,6 +101,7 @@
         greet((dp, (tp + k) % 8))
 
     mine, far = yh * 4 + x, (1 - yh) * 4 + x
+    text_copy.wait()
     text_vals = text_ref[...].astype(F32)
     text_inv = lax.rsqrt(jnp.sum(text_vals * text_vals, axis=1, keepdims=True) + EPS)
     text_nrm = text_vals * text_inv
@@ -218,9 +223,8 @@
         total = sums[:IMGS] + sums[IMGS:]
         return jnp.concatenate([total, total], axis=0)
 
-    scale = scale_ref[0]
-
     def loss(n):
+        scale = scale_ref[0]
         tm = tmean[...]
         own = ebuf[n, 0].astype(F32)
         for k in range(1, 8):
@@ -469,7 +473,7 @@
         gather_rest(msgs, msg_ss, msg_rs)
         all_msgs = msgs[...].reshape(256, D + HID + 256)
         tdir[...] = dot(all_msgs[:, D + HID:], all_msgs[:, :HALF], TN)
-        text_dir = scale * tdir[pl.ds(pl.multiple_of((core * 8 + mine) * 16, 16), 16), :]
+        text_dir = scale_ref[0] * tdir[pl.ds(pl.multiple_of((core * 8 + mine) * 16, 16), 16), :]
         text_dir = jnp.concatenate([text_dir[:IMGS], text_dir[IMGS:]], axis=1)
         vals = text_ref[...].astype(F32)
         t_inv = lax.rsqrt(jnp.sum(vals * vals, axis=1, keepdims=True) + EPS)
@@ -495,15 +499,17 @@
         square = jnp.concatenate([square, jnp.zeros((120, 256), F32)], axis=0)
         eg_t[...] = square.T
 
+    cs = jnp.zeros((16, HID), F32)
     for k in range(6):
         w_in_copy(k).wait()
+        cs = cs + dot(jnp.full((16, 256), 1.0, BF16), w_in[k * 256:(k + 1) * 256, :])
+    cs = cs[0:1]
 
     @pl.loop(2, CHUNKS)
     def _(c):
         tok_copy(c).start()
 
     w_out_copy.start()
-    cs = dot(jnp.full((16, D), 1.0, BF16), w_in[0:D, :])[0:1]
     csum[...] = cs
     w_in[D:D + 16, :] = split(cs)
     pl.semaphore_wait(barrier, 12)
@@ -534,6 +540,7 @@
             @pl.when(stage == 0)
             def _():
                 w_out_copy.wait()
+                labels_copy.wait()
 
             exchange_start(stage)
 
@@ -679,7 +686,6 @@
 
 def body(tokens, w_in, w_out, text_emb, labels, logit_scale, logit_bias):
     vmem = pl.BlockSpec(memory_space=pltpu.VMEM)
-    smem = pl.BlockSpec(memory_space=pltpu.SMEM)
     hbm = pl.BlockSpec(memory_space=pl.ANY)
     msg = D + HID + 256
     scratch = [
@@ -725,8 +731,10 @@
         pltpu.VMEM((96, HID), BF16),
         pltpu.VMEM((96, HID), BF16),
         pltpu.VMEM((IMGS, D), BF16),
+        pltpu.VMEM((IMGS, D), BF16),
+        pltpu.SMEM((IMGS,), jnp.int32),
         pltpu.SemaphoreType.DMA((CHUNKS,)),
-        pltpu.SemaphoreType.DMA((7,)),
+        pltpu.SemaphoreType.DMA((9,)),
         pltpu.SemaphoreType.DMA((8,)),
         pltpu.SemaphoreType.DMA((9,)),
         pltpu.SemaphoreType.DMA((GROUPS, 8)),
@@ -748,7 +756,7 @@
     results = pl.pallas_call(
         kernel,
         out_shape=shapes,
-        in_specs=[hbm, hbm, hbm, vmem, smem, smem, smem],
+        in_specs=[hbm] * 5 + [pl.BlockSpec(memory_space=pltpu.SMEM)] * 2,
         out_specs=(hbm, hbm, hbm, hbm),
         scratch_shapes=scratch,
         compiler_params=pltpu.CompilerParams(

time: 82.7 us -> 81.9 us (level)
  no operation moved by 1% of the time
where the time goes in v7:
time: 81.9 us; the launch traced here: 81.7 us
  Pallas kernels  79.8 us (97%)
  between operations  1.93 us (2%)
    pallas_call x1, Pallas kernels, body(): pl.pallas_call(kernel, out_shape=shapes, in_specs=[hbm] * 5 + [pl.BlockSp...  77.5 us
    pallas_call x1, Pallas kernels, body(): pl.pallas_call(hand_out, out_shape=shapes, in_specs=[vmem, vmem, vmem, vm...  2.21 us

profile of v7, /device:TPU:0, one launch (start us, length us, event | category | flops | bytes accessed | tf_op | source)
XLA Modules:
  0.0 81.7 jit_solution(8926665800102921980)
XLA Ops:
  1.9 77.5 %shard_map.102 = (bf16[192,2048]{1,0:T(8,128)(2,1)}, bf16[96,768]{1,0:T(8,128)(2,1)}, bf16[96,768]{1,0:T(8,128)(2,1)}, bf16[8,1536]{1,0:T(8,128)(2,1)}) custom-call(bf16[2048,1536]{1,0:T(8,128)(2,1)} %tokens_hbm.1, bf16[1536,768]{1,0:T(8,128)(2,1)} %w_in_hbm.1, bf16[768,1536]{1,0:T(8,128)(2,1)} %w_out_hbm.1, bf16[8,1536]{1,0:T(8,128)(2,1)} %text_hbm.1, ...), custom_call_target="tpu_custom_call" | custom-call | flops 14495514624 | bytes 14680064 | tf_op jit(solution)/shard_map/pallas_call | solution.py:756
  79.5 2.2 %shard_map.103 = (bf16[192,2048]{1,0:T(8,128)(2,1)}, bf16[96,768]{1,0:T(8,128)(2,1)}, bf16[96,768]{1,0:T(8,128)(2,1)}, bf16[8,1536]{1,0:T(8,128)(2,1)}) custom-call(bf16[192,2048]{1,0:T(8,128)(2,1)} %get-tuple-element.12.a, bf16[96,768]{1,0:T(8,128)(2,1)} %get-tuple-element.13.b, bf16[96,768]{1,0:T(8,128)(2,1)} %get-tuple-element.14.c, ...), custom_call_target="tpu_custom_call" | custom-call | bytes 2097152 | tf_op jit(solution)/shard_map/pallas_call | solution.py:769
